TPU v7x, 512 devices: a whole 4x4x16 slice. The times are simulated.
512 devices in a mesh: ctx: 64 (over x, z), head: 8 (over y, core).
Axes of the slice: x: 4, y: 4, z: 16, core: 2. Of those that a mesh axis runs over, the one named last changes fastest.
Arguments:
- queries: bfloat16 [65536, 4096], P(('ctx', 'head')), may hold values from -6 to 6
- keys: bfloat16 [65536, 1024], P(('ctx', 'head')), may hold values from -6 to 6
- values: bfloat16 [65536, 1024], P(('ctx', 'head')), may hold values from -6 to 6
- doc_ids: int32 [65536], P('ctx'), may hold values from 0 to 127, never falling along the last dimension, each value on 1 to 1024 neighbouring positions
- sample_rows: int32 [4096], P('ctx'), may hold values from 0 to 1023, as said below
- owners: int32 [4096, 1], P('ctx'), may hold values from 0 to 63; in each aligned block of 64 rows (0 to 63, 64 to 127, ...) at most 2 rows name the same one
- targets: int32 [4096, 2], P('ctx'), may hold values from 0 to 2047
- in_proj: bfloat16 [4096, 1024], P('head'), may hold values from -0.09375 to 0.09375
- dec_gain: float32 [1024], replicated, may hold values from 0.5 to 1.5
- code_heads: bfloat16 [2, 1024, 2048], P(None, None, 'head'), may hold values from -32 to 32
Outputs:
- attended: bfloat16 [65536, 4096], P('ctx', 'head')
- slot_loss: float32 [64, 128], P('ctx')
Inputs may be any that keep to these rules, and one draw needn't show every extreme that they name: `sample_rows`: entry j of one ctx index's list lies in the j-th aligned group of 16 frames of its block. `owners`: within the 64 entries of one ctx index at most 2 name one owner. `doc_ids`: never falling; each document 1 to 1024 frames, one exactly 1024.
All inputs are finite; a program needn't handle non-finite values.
Results may differ from a plain program's by a relative error of at most 0.0036.
Values may be sent and summed in bfloat16 or wider, within the bound.
No kernel may reach another device: no remote copies, remote signals or barrier semaphores. Data moves between devices by JAX's collectives and lax.ppermute only.
A program may use at most 64 MiB of HBM per device.

v0:
```python
import math

import jax
import jax.numpy as jnp
from jax import lax
from jax.sharding import PartitionSpec as P

HEAD_SIZE = 128


def from_behind(value, axis, steps):
    count = lax.axis_size(axis)
    first, last = (max(0, -steps), min(count, count - steps))
    return lax.ppermute(value, axis, [(source, source + steps) for source in range(first, last)])


def block_scores(query_tile, key_tile, score_scale):
    return (
        jnp.einsum("qgd,kd->qgk", query_tile, key_tile, preferred_element_type=jnp.float32)
        * score_scale
    )


def local(
    queries, keys, values, doc_ids, sample_rows, owners, targets, in_proj, dec_gain, code_heads
):
    queries_here, keys_here, values_here = (
        lax.all_to_all(queries, "head", split_axis=1, concat_axis=0, tiled=True),
        lax.all_to_all(keys, "head", split_axis=1, concat_axis=0, tiled=True),
        lax.all_to_all(values, "head", split_axis=1, concat_axis=0, tiled=True),
    )
    marked_docs = doc_ids + 1
    keys_before, values_before, docs_before = from_behind(
        (keys_here, values_here, marked_docs), "ctx", 1
    )
    block_rows = queries_here.shape[0]
    key_rows = 2 * block_rows
    all_keys = jnp.concatenate([keys_before, keys_here], axis=0)
    all_values = jnp.concatenate([values_before, values_here], axis=0)
    all_docs = jnp.concatenate([docs_before, marked_docs])
    key_places = jnp.arange(key_rows, dtype=jnp.int32) - block_rows
    kv_heads = keys_here.shape[1] // HEAD_SIZE
    group_width = queries_here.shape[1] // HEAD_SIZE // kv_heads
    query_tile = min(128, block_rows)
    tile_total = block_rows // query_tile
    score_scale = 1.0 / math.sqrt(HEAD_SIZE)
    offsets = jnp.arange(tile_total, dtype=jnp.int32) * query_tile
    head_keys = all_keys
    head_values = all_values
    head_queries = queries_here.reshape(tile_total, query_tile, group_width, HEAD_SIZE)

    def one_tile(operands, head_keys=head_keys, head_values=head_values):
        tile_queries, start_shift = operands
        query_places = start_shift + jnp.arange(query_tile, dtype=jnp.int32)
        query_docs = lax.dynamic_slice_in_dim(marked_docs, start_shift, query_tile, 0)
        visible = (query_docs[:, None] == all_docs[None, :]) & (
            key_places[None, :] <= query_places[:, None]
        )
        scores = block_scores(tile_queries, head_keys, score_scale)
        scores = jnp.where(visible[:, None, :], scores, -1e30)
        highest = jnp.max(scores, axis=-1, keepdims=True)
        weights = jnp.exp(scores - highest)
        totals = jnp.sum(weights, axis=-1, keepdims=True)
        rounded = weights.astype(jnp.bfloat16)
        mixed = (
            jnp.einsum("qgk,kd->qgd", rounded, head_values, preferred_element_type=jnp.float32)
            / totals
        )
        return mixed.astype(jnp.bfloat16).reshape(query_tile, group_width * HEAD_SIZE)

    result = lax.map(one_tile, (head_queries, offsets))
    pieces = result.reshape(block_rows, group_width * HEAD_SIZE)
    ctx_count = lax.axis_size("ctx")
    head_number = lax.axis_index("head")
    owner_ids = owners[:, 0]
    sampled = owner_ids.shape[0]
    capacity = max(2, 2 * sampled // ctx_count)
    slot_count = ctx_count * capacity
    positions = jnp.arange(sampled, dtype=jnp.int32)
    before_same = (owner_ids[None, :] == owner_ids[:, None]) & (
        positions[None, :] < positions[:, None]
    )
    ranks = jnp.sum(before_same.astype(jnp.int32), axis=1)
    slot_of = owner_ids * capacity + ranks
    placing = jnp.arange(slot_count, dtype=jnp.int32)[:, None] == slot_of[None, :]
    features = jnp.take(pieces, sample_rows, axis=0)
    bucket = jnp.dot(
        placing.astype(jnp.bfloat16), features, preferred_element_type=jnp.float32
    ).astype(jnp.bfloat16)
    target_slots = (
        jnp.dot(
            placing.astype(jnp.float32),
            (targets + 1).astype(jnp.float32),
            precision=lax.Precision.HIGHEST,
        ).astype(jnp.int32)
        - 1
    )
    arrived, arrived_targets = (
        lax.all_to_all(bucket, "ctx", split_axis=0, concat_axis=0, tiled=True),
        lax.all_to_all(target_slots, "ctx", split_axis=0, concat_axis=0, tiled=True),
    )
    decoder_state = lax.psum(jnp.dot(arrived, in_proj, preferred_element_type=jnp.float32), "head")
    normed = (
        decoder_state
        * lax.rsqrt(jnp.mean(decoder_state * decoder_state, axis=-1, keepdims=True) + 1e-06)
        * dec_gain
    ).astype(jnp.bfloat16)
    logits = jnp.einsum("sd,cdv->scv", normed, code_heads, preferred_element_type=jnp.float32)
    vocab_slice = logits.shape[2]
    code_index = head_number * vocab_slice + jnp.arange(vocab_slice, dtype=jnp.int32)
    target_hit = code_index[None, None, :] == arrived_targets[:, :, None]
    target_logit = jnp.sum(jnp.where(target_hit, logits, 0.0), axis=-1)
    local_top = jnp.max(logits, axis=-1)
    row_top = lax.pmax(local_top, "head")
    row_mass, row_target = lax.psum(
        (jnp.sum(jnp.exp(logits - row_top[..., None]), axis=-1), target_logit), "head"
    )
    frame_loss = jnp.log(row_mass) + row_top - row_target
    slot_loss = jnp.where(arrived_targets[:, 0] >= 0, jnp.mean(frame_loss, axis=1), 0.0)
    return (pieces, slot_loss[None, :])


def solution(mesh):
    in_specs = (
        P(("ctx", "head"), None),
        P(("ctx", "head"), None),
        P(("ctx", "head"), None),
        P("ctx"),
        P("ctx"),
        P("ctx", None),
        P("ctx", None),
        P("head", None),
        P(),
        P(None, None, "head"),
    )
    out_specs = (P("ctx", "head"), P("ctx", None))
    return jax.shard_map(local, mesh=mesh, in_specs=in_specs, out_specs=out_specs, check_vma=False)
```

profile of v0, /device:TPU:1, one launch (start us, length us, event | category | flops | bytes accessed | tf_op | source)
XLA Modules:
  0.0 265.3 jit_solution(5673214661518338516)
XLA Ops:
  8.0 4.4 %collective-permute-start = (s32[1024]{0:T(1024)S(1)}, s32[1024]{0:T(1024)S(1)}, u32[]{:S(2)}, u32[]{:S(2)}) collective-permute-start(s32[1024]{0:T(1024)S(1)} %broadcast_add_fusion), channel_id=1, source_target_pairs={{0,8},{8,16},{16,24},{24,32},{32,40},{40,48},{48,56},{56,64},{64,7... | collective-permute-start | bytes 12296 | tf_op jit(solution)/shard_map/ppermute | solution.py:14
  12.4 1.8 copy.38
  14.1 7.1 %all-to-all-start.2 = ((bf16[128,8,128]{0,2,1:T(8,128)(2,1)}), bf16[128,8,128]{0,2,1:T(8,128)(2,1)S(1)}, u32[]{:S(2)}, u32[]{:S(2)}) async-start(bf16[128,8,128]{0,2,1:T(8,128)(2,1)} %bitcast.5), calls=%async_computation.2 | async-start | bytes 524288 | tf_op jit(solution)/shard_map/all_to_all | solution.py:30
  21.2 1.7 copy_bitcast_fusion
  23.6 4.2 %all-to-all-done.2 = bf16[128,8,128]{0,2,1:T(8,128)(2,1)S(1)} async-done(((bf16[128,8,128]{0,2,1:T(8,128)(2,1)}), bf16[128,8,128]{0,2,1:T(8,128)(2,1)S(1)}, u32[]{:S(2)}, u32[]{:S(2)}) %all-to-all-start.2) | async-done | bytes 262176 | tf_op jit(solution)/shard_map/all_to_all | solution.py:30
  27.8 4.4 %all-to-all-start.1 = ((bf16[128,8,128]{2,0,1:T(8,128)(2,1)}), bf16[128,8,128]{2,0,1:T(8,128)(2,1)S(1)}, u32[]{:S(2)}, u32[]{:S(2)}) async-start(bf16[128,8,128]{2,0,1:T(8,128)(2,1)} %copy_bitcast_fusion), calls=%async_computation.1 | async-start | bytes 524288 | tf_op jit(solution)/shard_map/all_to_all | solution.py:29
  33.0 2.3 copy.36
  35.3 3.3 %all-to-all-done.1 = bf16[128,8,128]{2,0,1:T(8,128)(2,1)S(1)} async-done(((bf16[128,8,128]{2,0,1:T(8,128)(2,1)}), bf16[128,8,128]{2,0,1:T(8,128)(2,1)S(1)}, u32[]{:S(2)}, u32[]{:S(2)}) %all-to-all-start.1) | async-done | bytes 262176 | tf_op jit(solution)/shard_map/all_to_all | solution.py:29
  38.6 4.5 %all-to-all-start = ((bf16[128,8,512]{0,2,1:T(8,128)(2,1)}), bf16[128,8,512]{0,2,1:T(8,128)(2,1)S(1)}, u32[]{:S(2)}, u32[]{:S(2)}) async-start(bf16[128,8,512]{0,2,1:T(8,128)(2,1)} %bitcast), calls=%async_computation | async-start | bytes 2097152 | tf_op jit(solution)/shard_map/all_to_all | solution.py:28
  43.4 2.6 collective-permute-start.2
  45.9 3.6 %collective-permute-start.1 = (bf16[1024,128]{1,0:T(8,128)(2,1)S(1)}, bf16[1024,128]{1,0:T(8,128)(2,1)}, u32[]{:S(2)}, u32[]{:S(2)}) collective-permute-start(bf16[1024,128]{1,0:T(8,128)(2,1)S(1)} %bitcast.63), channel_id=1, source_target_pairs={{0,8},{8,16},{16,24},{24,32},{32,40},{40,48},{48,56},{56,64},{64,7... | collective-permute-start | bytes 786440 | tf_op jit(solution)/shard_map/ppermute | solution.py:14
  49.5 1.2 collective-permute-done.2
  52.0 4.4 %collective-permute-done.1 = bf16[1024,128]{1,0:T(8,128)(2,1)} collective-permute-done((bf16[1024,128]{1,0:T(8,128)(2,1)S(1)}, bf16[1024,128]{1,0:T(8,128)(2,1)}, u32[]{:S(2)}, u32[]{:S(2)}) %collective-permute-start.1) | collective-permute-done | bytes 262176 | tf_op jit(solution)/shard_map/ppermute | solution.py:14
  58.3 64.3 %while.11 = (s32[]{:T(128)}, bf16[8,128,512]{2,1,0:T(8,128)(2,1)}, s32[8]{0:T(128)S(1)}, s32[1024]{0:T(1024)S(1)}, s32[2048]{0:T(1024)S(1)}, /*index=5*/bf16[8,1...) while((s32[]{:T(128)}, bf16[8,128,512]{2,1,0:T(8,128)(2,1)}, ...), condition=%wide.region_3.4_spmd.clone, body=%wide.region_0.3_spmd.clone.sunk | while | flops 549323904 | bytes 15504551 | solution.py:71
  64.3 1.2 fusion.54
  72.3 1.2 fusion.54
  80.3 1.2 fusion.54
  88.4 1.2 fusion.54
  96.4 1.2 fusion.54
  104.5 1.2 fusion.54
  112.5 1.2 fusion.54
  120.6 1.2 fusion.54
  122.6 2.2 gather_fusion
  125.1 32.1 %all_to_all.78 = bf16[64,2,512]{2,1,0:T(2,128)(2,1)S(1)} all-to-all(bf16[64,2,512]{2,1,0:T(2,128)(2,1)S(1)} %all_to_all.70), channel_id=1, replica_groups=mesh['ctx'=64,'head'=8] {'ctx'}, dimensions={0} | all-to-all | bytes 262144 | tf_op jit(solution)/shard_map/all_to_all | solution.py:99
  157.3 1.1 fusion.40
  159.5 7.4 %all-to-all-start.3 = ((s32[64,2,2]{1,2,0:T(2,128)}), s32[64,2,2]{1,2,0:T(2,128)S(1)}, u32[]{:S(2)}, u32[]{:S(2)}) async-start(s32[64,2,2]{1,2,0:T(2,128)} %copy.43), calls=%async_computation.3 | async-start | bytes 131072 | tf_op jit(solution)/shard_map/all_to_all | solution.py:100
  166.9 13.5 %all-to-all-done.3 = s32[64,2,2]{1,2,0:T(2,128)S(1)} async-done(((s32[64,2,2]{1,2,0:T(2,128)}), s32[64,2,2]{1,2,0:T(2,128)S(1)}, u32[]{:S(2)}, u32[]{:S(2)}) %all-to-all-start.3) | async-done | bytes 1056 | tf_op jit(solution)/shard_map/all_to_all | solution.py:100
  180.6 46.7 %all-reduce.3.cloned.1.call-done = f32[128,1024]{1,0:T(8,128)} async-done(((f32[128,1024]{1,0:T(8,128)}), f32[128,1024]{1,0:T(8,128)}) %all-reduce.3.cloned.1.call-update) | async-done | bytes 524304 | tf_op jit(solution)/shard_map/psum | solution.py:102
  227.2 1.2 multiply_reduce_fusion
  228.4 1.5 fusion.39
  229.9 14.0 %pmax.7 = f32[128,2]{0,1:T(2,128)S(1)} all-reduce(f32[128,2]{0,1:T(2,128)S(1)} %get-tuple-element.122), channel_id=1, replica_groups=mesh['ctx'=64,'head'=8] {'head'}, use_global_device_ids=true, to_apply=%region_8.9 | all-reduce | flops 256 | bytes 2048 | tf_op jit(solution)/shard_map/pmax | solution.py:114
  244.1 13.8 %all-reduce = (f32[128,2]{0,1:T(2,128)S(1)}, f32[128,2]{0,1:T(2,128)S(1)}) all-reduce(f32[128,2]{0,1:T(2,128)S(1)} %get-tuple-element.101, f32[128,2]{0,1:T(2,128)S(1)} %get-tuple-element.100), channel_id=1, replica_groups=mesh['ctx'=64,'head'=8] {'head'}, use_global_device_ids=true, to_apply=%region_12.13 | all-reduce | flops 512 | bytes 4096 | tf_op jit(solution)/shard_map/psum | solution.py:115
  (114 shorter events, 45.5 us)
Async XLA Ops:
  7.2 150.1 %copy-start = (bf16[512,1024]{1,0:T(8,128)(2,1)S(1)}, bf16[512,1024]{1,0:T(8,128)(2,1)}, u32[]{:S(2)}) copy-start(bf16[512,1024]{1,0:T(8,128)(2,1)} %param.19) | copy-start | bytes 3145732
  7.2 36.0 %copy-start.5 = (s32[64]{0:T(128)S(1)}, s32[64]{0:T(128)}, u32[]{:S(2)}) copy-start(s32[64]{0:T(128)} %param.16) | copy-start | bytes 772
  7.2 28.1 %copy-start.4 = (s32[64,1]{0,1:T(1,128)S(1)}, s32[64,1]{0,1:T(1,128)}, u32[]{:S(2)}) copy-start(s32[64,1]{0,1:T(1,128)} %param.17) | copy-start | bytes 772
  8.0 41.5 %collective-permute-start = (s32[1024]{0:T(1024)S(1)}, s32[1024]{0:T(1024)S(1)}, u32[]{:S(2)}, u32[]{:S(2)}) collective-permute-start(s32[1024]{0:T(1024)S(1)} %broadcast_add_fusion), channel_id=1, source_target_pairs={{0,8},{8,16},{16,24},{24,32},{32,40},{40,48},{48,56},{56,64},{64,7... | collective-permute-start | bytes 12296 | tf_op jit(solution)/shard_map/ppermute | solution.py:14
  14.1 13.6 %all-to-all-start.2 = ((bf16[128,8,128]{0,2,1:T(8,128)(2,1)}), bf16[128,8,128]{0,2,1:T(8,128)(2,1)S(1)}, u32[]{:S(2)}, u32[]{:S(2)}) async-start(bf16[128,8,128]{0,2,1:T(8,128)(2,1)} %bitcast.5), calls=%async_computation.2 | async-start | bytes 524288 | tf_op jit(solution)/shard_map/all_to_all | solution.py:30
  27.8 10.9 %all-to-all-start.1 = ((bf16[128,8,128]{2,0,1:T(8,128)(2,1)}), bf16[128,8,128]{2,0,1:T(8,128)(2,1)S(1)}, u32[]{:S(2)}, u32[]{:S(2)}) async-start(bf16[128,8,128]{2,0,1:T(8,128)(2,1)} %copy_bitcast_fusion), calls=%async_computation.1 | async-start | bytes 524288 | tf_op jit(solution)/shard_map/all_to_all | solution.py:29
  38.6 19.6 %all-to-all-start = ((bf16[128,8,512]{0,2,1:T(8,128)(2,1)}), bf16[128,8,512]{0,2,1:T(8,128)(2,1)S(1)}, u32[]{:S(2)}, u32[]{:S(2)}) async-start(bf16[128,8,512]{0,2,1:T(8,128)(2,1)} %bitcast), calls=%async_computation | async-start | bytes 2097152 | tf_op jit(solution)/shard_map/all_to_all | solution.py:28
  43.1 184.1 %all-reduce.3.cloned.1.call-start = ((), (), s32[]{:S(2)}) async-start(), calls=%async_computation.5 | async-start | bytes 1048576 | tf_op jit(solution)/shard_map/psum | solution.py:102
  43.4 7.4 %collective-permute-start.2 = (bf16[1024,128]{1,0:T(8,128)(2,1)S(1)}, bf16[1024,128]{1,0:T(8,128)(2,1)}, u32[]{:S(2)}, u32[]{:S(2)}) collective-permute-start(bf16[1024,128]{1,0:T(8,128)(2,1)S(1)} %bitcast.65), channel_id=1, source_target_pairs={{0,8},{8,16},{16,24},{24,32},{32,40},{40,48},{48,56},{56,64},{64,7... | collective-permute-start | bytes 786440 | tf_op jit(solution)/shard_map/ppermute | solution.py:14
  45.9 10.4 %collective-permute-start.1 = (bf16[1024,128]{1,0:T(8,128)(2,1)S(1)}, bf16[1024,128]{1,0:T(8,128)(2,1)}, u32[]{:S(2)}, u32[]{:S(2)}) collective-permute-start(bf16[1024,128]{1,0:T(8,128)(2,1)S(1)} %bitcast.63), channel_id=1, source_target_pairs={{0,8},{8,16},{16,24},{24,32},{32,40},{40,48},{48,56},{56,64},{64,7... | collective-permute-start | bytes 786440 | tf_op jit(solution)/shard_map/ppermute | solution.py:14
  58.3 100.2 %copy-start.3 = (s32[64,2]{0,1:T(2,128)S(1)}, s32[64,2]{0,1:T(2,128)}, u32[]{:S(2)}) copy-start(s32[64,2]{0,1:T(2,128)} %param.18) | copy-start | bytes 1540
  122.6 105.8 %copy-start.1 = (bf16[2,1024,256]{2,1,0:T(8,128)(2,1)S(1)}, bf16[2,1024,256]{2,1,0:T(8,128)(2,1)}, u32[]{:S(2)}) copy-start(bf16[2,1024,256]{2,1,0:T(8,128)(2,1)} %param.21) | copy-start | bytes 3145732
  122.6 105.8 %copy-start.2 = (f32[1024]{0:T(1024)S(1)}, f32[1024]{0:T(1024)}, u32[]{:S(2)}) copy-start(f32[1024]{0:T(1024)} %param.20) | copy-start | bytes 12292
  159.5 21.0 %all-to-all-start.3 = ((s32[64,2,2]{1,2,0:T(2,128)}), s32[64,2,2]{1,2,0:T(2,128)S(1)}, u32[]{:S(2)}, u32[]{:S(2)}) async-start(s32[64,2,2]{1,2,0:T(2,128)} %copy.43), calls=%async_computation.3 | async-start | bytes 131072 | tf_op jit(solution)/shard_map/all_to_all | solution.py:100
Sparse Core Ops, SparseCore 0:
  158.6 68.6 all-reduce.2
where the time goes:
time: 266 us; the launch traced here: 265 us
  waiting for transfers between devices  74.2 us (28%)
  blocking collectives  59.9 us (23%)
  starting transfers between devices  33.9 us (13%)
  other arithmetic  23.1 us (9%)
  local copies, waits for them, and re-layouts  21.7 us (8%)
  matrix products  21.4 us (8%)
  loops' own time  16.9 us (6%)
  between operations  14.2 us (5%)
    psum x1, waiting for transfers between devices, local(): lax.psum(jnp.dot(arrived, in_proj, preferred_element_type=jnp.float32), '...  46.7 us
    all_to_all x1, blocking collectives, local(): lax.all_to_all(bucket, 'ctx', split_axis=0, concat_axis=0, tiled=True)  32.1 us
    another operation x1, loops' own time, local(): result = lax.map(one_tile, (head_queries, offsets))  16.9 us
    pmax x1, blocking collectives, local(): row_top = lax.pmax(local_top, 'head')  14 us
    psum x1, blocking collectives, local(): lax.psum((jnp.sum(jnp.exp(logits - row_top[..., None]), axis=-1), target_...  13.8 us
    all_to_all x1, waiting for transfers between devices, local(): lax.all_to_all(target_slots, 'ctx', split_axis=0, concat_axis=0, tiled=True)  13.5 us
    ppermute x3, starting transfers between devices, from_behind(): lax.ppermute(value, axis, [(source, source + steps) for source in range(f...  10.5 us
    dot_general x8, matrix products, one_tile(): jnp.einsum('qgk,kd->qgd', rounded, head_values, preferred_element_type=jn...  9.96 us
  transfers between devices with their start and end apart: 8, of which 7 were waited for; matrix products, arithmetic and copies ran while one was open for 4% of the time, Pallas kernels for 0%

commit v1 on v0

v1 whole, which is shorter than its diff:
```python
import functools
import math

import jax
import jax.numpy as jnp
from jax import lax
from jax.experimental import pallas as pl
from jax.experimental.pallas import tpu as pltpu
from jax.sharding import PartitionSpec as P

HEAD_SIZE = 128
KEY_TILE = 256
MASKED = -1e30
bf16 = jnp.bfloat16
f32 = jnp.float32
VMEM = pl.BlockSpec(memory_space=pltpu.VMEM)
SMEM = pl.BlockSpec(memory_space=pltpu.SMEM)
ANY = pl.BlockSpec(memory_space=pl.ANY)


def params(mib=48):
    return pltpu.CompilerParams(vmem_limit_bytes=mib * 2**20)


def cost(flops, moved, exps=0):
    return pl.CostEstimate(flops=flops, bytes_accessed=moved, transcendentals=exps)


def shape_of(shape, dtype):
    return jax.ShapeDtypeStruct(shape, dtype)


def pack_kernel(
    group, rows_ref, keys_hbm, values_hbm, queries_hbm, out_ref, keys_ref, values_ref, queries_ref, sems
):
    heads = out_ref.shape[0]
    frames = keys_ref.shape[0]
    per_head = rows_ref.shape[0] // heads
    pieces = queries_ref.shape[0] // 32
    copies = []
    for p in range(pieces):
        rows = pl.ds(p * 32, 32)
        copies.append(
            pltpu.make_async_copy(queries_hbm.at[rows], queries_ref.at[rows], sems.at[p])
        )
    copies.append(pltpu.make_async_copy(keys_hbm, keys_ref, sems.at[pieces]))
    copies.append(pltpu.make_async_copy(values_hbm, values_ref, sems.at[pieces + 1]))
    for copy in copies:
        copy.start()
    me = lax.axis_index("head")
    row = lax.broadcasted_iota(jnp.int32, (per_head, frames), 0)
    lane = lax.broadcasted_iota(jnp.int32, (per_head, frames), 1)
    wanted = jnp.full((per_head, frames), -1, jnp.int32)
    for i in range(per_head):
        wanted = jnp.where(row == i, rows_ref[me * per_head + i] - me * frames, wanted)
    chosen = jnp.where(lane == wanted, 1.0, 0.0).astype(bf16)
    for copy in copies:
        copy.wait()
    picked = jnp.dot(chosen, queries_ref[...], preferred_element_type=f32)
    for g in range(heads):
        span = pl.ds(g * HEAD_SIZE, HEAD_SIZE)
        out_ref[g, pl.ds(0, frames), :] = keys_ref[:, span]
        out_ref[g, pl.ds(frames, frames), :] = values_ref[:, span]
        parts = [
            picked[:, (g * group + j) * HEAD_SIZE : (g * group + j + 1) * HEAD_SIZE]
            for j in range(group)
        ]
        out_ref[g, pl.ds(2 * frames, group * per_head), :] = jnp.concatenate(parts, axis=0).astype(
            bf16
        )


def block_rows(s, own_ref, first_ref, second_ref, frames, which):
    heads = own_ref.shape[0]
    half = heads // 2
    if s >= heads:
        return own_ref[s - heads, pl.ds(which * frames, frames), :]
    ref, at = (first_ref, s) if s < half else (second_ref, s - half)
    return ref[pl.ds((2 * at + which) * frames, frames), :]


def doc_rows(second_ref, docs_ref, frames):
    count = docs_ref.shape[0]
    before = second_ref[pl.ds(count * frames, 2 * count), :].astype(f32)[:count]
    return jnp.concatenate([before, docs_ref[...]], axis=0)


def unpack_kernel(
    own_ref, first_ref, second_ref, docs_ref, marks_ref, keys_ref, values_ref, all_docs_ref, low_ref
):
    heads = own_ref.shape[0]
    frames = docs_ref.shape[1]
    one = jnp.ones((frames, HEAD_SIZE), bf16)
    for s in range(2 * heads):
        rows = pl.ds(s * frames, frames)
        keys_ref[rows, :] = block_rows(s, own_ref, first_ref, second_ref, frames, 0)
        values_ref[rows, pl.ds(0, HEAD_SIZE)] = block_rows(
            s, own_ref, first_ref, second_ref, frames, 1
        )
        values_ref[rows, pl.ds(HEAD_SIZE, HEAD_SIZE)] = one
    docs = doc_rows(second_ref, docs_ref, frames)
    all_docs_ref[...] = docs
    for t in range(low_ref.shape[0]):
        below = jnp.where(docs < marks_ref[t].astype(f32), 1.0, 0.0)
        low_ref[t] = jnp.sum(below).astype(jnp.int32) // KEY_TILE


def sample_kernel(
    scale, own_ref, first_ref, second_ref, docs_ref, mine_ref, proj_ref, out_ref, scores_ref
):
    heads = own_ref.shape[0]
    frames = docs_ref.shape[1]
    extra = own_ref.shape[1] - 2 * frames
    group = proj_ref.shape[0] // HEAD_SIZE
    per_head = extra // group
    rows = heads * extra
    tile = 2 * frames
    queries = own_ref[:, pl.ds(2 * frames, extra), :].reshape(rows, HEAD_SIZE)
    docs = doc_rows(second_ref, docs_ref, frames)
    my_doc = jnp.broadcast_to(mine_ref[:, 0:1], (rows, tile))
    my_place = jnp.broadcast_to(mine_ref[:, 1:2], (rows, tile))
    lane = lax.broadcasted_iota(jnp.int32, (rows, tile), 1).astype(f32)
    highest = jnp.full((rows, HEAD_SIZE), MASKED, f32)
    for s in range(0, 2 * heads, 2):
        key_tile = jnp.concatenate(
            [block_rows(s + i, own_ref, first_ref, second_ref, frames, 0) for i in range(2)], axis=0
        )
        scores = lax.dot_general(
            queries, key_tile, (((1,), (1,)), ((), ())), preferred_element_type=f32
        )
        tile_docs = jnp.concatenate([docs[s : s + 1], docs[s + 1 : s + 2]], axis=1)
        seen = (tile_docs == my_doc) & (lane <= my_place - s * frames)
        scores = jnp.where(seen, scores * scale, MASKED)
        start = s * frames
        scores_ref[:, start : start + tile] = scores
        for part in range(tile // HEAD_SIZE):
            highest = jnp.maximum(highest, scores[:, part * HEAD_SIZE : (part + 1) * HEAD_SIZE])
    top = jnp.max(highest, axis=1, keepdims=True)
    total = jnp.zeros((rows, HEAD_SIZE), f32)
    mixed = jnp.zeros((rows, HEAD_SIZE), f32)
    for s in range(0, 2 * heads, 2):
        value_tile = jnp.concatenate(
            [block_rows(s + i, own_ref, first_ref, second_ref, frames, 1) for i in range(2)], axis=0
        )
        start = s * frames
        weights = jnp.exp2(scores_ref[:, start : start + tile] - top)
        for part in range(tile // HEAD_SIZE):
            total = total + weights[:, part * HEAD_SIZE : (part + 1) * HEAD_SIZE]
        mixed = mixed + jnp.dot(weights.astype(bf16), value_tile, preferred_element_type=f32)
    attended = mixed / jnp.sum(total, axis=1, keepdims=True)
    by_group = attended.reshape(heads, group, per_head, HEAD_SIZE)
    state = jnp.zeros((heads * per_head, proj_ref.shape[1]), f32)
    for j in range(group):
        part = by_group[:, j].reshape(heads * per_head, HEAD_SIZE).astype(bf16)
        state = state + jnp.dot(
            part, proj_ref[pl.ds(j * HEAD_SIZE, HEAD_SIZE), :], preferred_element_type=f32
        )
    state = state.astype(bf16)
    for d in range(heads):
        out_ref[d] = state


def logits_kernel(parts_ref, gain_ref, codes_ref, targets_ref, out_ref):
    heads, samples, width = parts_ref.shape
    books, _, codes = codes_ref.shape
    state = parts_ref[0].astype(f32)
    for s in range(1, heads):
        state = state + parts_ref[s].astype(f32)
    square = jnp.sum(state * state, axis=1, keepdims=True)
    normed = (state * lax.rsqrt(square / width + 1e-06) * gain_ref[...]).astype(bf16)
    lane = lax.broadcasted_iota(jnp.int32, (samples, 128), 1)
    code = lax.broadcasted_iota(jnp.int32, (samples, codes), 1)
    stats = jnp.zeros((samples, 128), f32)
    for b in range(books):
        logits = jnp.dot(normed, codes_ref[b], preferred_element_type=f32)
        top = jnp.max(logits, axis=1, keepdims=True)
        mass = jnp.sum(jnp.exp(logits - top), axis=1, keepdims=True)
        hit = code == targets_ref[:, b : b + 1]
        target = jnp.sum(jnp.where(hit, logits, 0.0), axis=1, keepdims=True)
        for k, column in enumerate((top, mass, target)):
            stats = jnp.where(lane == 3 * b + k, column, stats)
    padded = jnp.concatenate([stats, jnp.zeros((128 - samples, 128), f32)], axis=0)
    across = jnp.transpose(padded)[:8]
    for d in range(heads):
        out_ref[d] = across


def place_kernel(books, stats_ref, owner_ref, column_ref, out_ref):
    heads = stats_ref.shape[0]
    loss = jnp.zeros((1, 128), f32)
    for b in range(books):
        tops = [stats_ref[s, 3 * b : 3 * b + 1, :] for s in range(heads)]
        top = functools.reduce(jnp.maximum, tops)
        mass = jnp.zeros((1, 128), f32)
        target = jnp.zeros((1, 128), f32)
        for s in range(heads):
            mass = mass + stats_ref[s, 3 * b + 1 : 3 * b + 2, :] * jnp.exp(tops[s] - top)
            target = target + stats_ref[s, 3 * b + 2 : 3 * b + 3, :]
        loss = loss + (jnp.log(mass) + top - target)
    loss = loss * (1.0 / books)
    spread = jnp.where(owner_ref[...] > 0.0, loss, 0.0)
    out_ref[...] = jnp.dot(
        spread, column_ref[...], preferred_element_type=f32, precision=lax.Precision.HIGHEST
    )


def main_kernel(scale, first_tile, low_ref, queries_ref, keys_ref, values_ref, docs_ref, across_ref, *refs):
    out_ref, bias_ref, scores_ref = refs[-3:]
    tile, width = queries_ref.shape
    group = width // HEAD_SIZE
    block = keys_ref.shape[0] // 2
    number = first_tile + pl.program_id(0)
    start = block + number * tile
    low = low_ref[number]
    high = (start + tile + KEY_TILE - 1) // KEY_TILE
    halves = KEY_TILE // HEAD_SIZE

    def body(count):
        base = pl.multiple_of(low * KEY_TILE, KEY_TILE)
        my_doc = jnp.broadcast_to(docs_ref[...], (tile, HEAD_SIZE))
        ahead = lax.broadcasted_iota(jnp.int32, (tile, HEAD_SIZE), 0) - lax.broadcasted_iota(
            jnp.int32, (tile, HEAD_SIZE), 1
        )
        for k in range(count * halves):
            doc = across_ref[pl.ds(low * halves + k, 1), :]
            seen = (doc == my_doc) & (ahead >= base + k * HEAD_SIZE - start)
            bias_ref[:, k * HEAD_SIZE : (k + 1) * HEAD_SIZE] = jnp.where(seen, 0.0, MASKED)
        for j in range(group):
            queries = queries_ref[:, j * HEAD_SIZE : (j + 1) * HEAD_SIZE]
            highest = jnp.full((tile, HEAD_SIZE), MASKED, f32)
            for k in range(count):
                span = slice(k * KEY_TILE, (k + 1) * KEY_TILE)
                key_tile = keys_ref[pl.ds(base + k * KEY_TILE, KEY_TILE), :]
                scores = lax.dot_general(
                    queries, key_tile, (((1,), (1,)), ((), ())), preferred_element_type=f32
                )
                scores = scores * scale + bias_ref[:, span]
                scores_ref[j, :, span] = scores
                highest = jnp.maximum(
                    highest, jnp.maximum(scores[:, :HEAD_SIZE], scores[:, HEAD_SIZE:])
                )
            top = jnp.max(highest, axis=1, keepdims=True)
            mixed = None
            for k in range(count):
                span = slice(k * KEY_TILE, (k + 1) * KEY_TILE)
                weights = jnp.exp2(scores_ref[j, :, span] - top).astype(bf16)
                value_tile = values_ref[pl.ds(base + k * KEY_TILE, KEY_TILE), :]
                part = jnp.dot(weights, value_tile, preferred_element_type=f32)
                mixed = part if mixed is None else mixed + part
            out_ref[:, j * HEAD_SIZE : (j + 1) * HEAD_SIZE] = (
                mixed[:, :HEAD_SIZE] / mixed[:, HEAD_SIZE:]
            ).astype(bf16)

    most = scores_ref.shape[2] // KEY_TILE
    for count in range(1, most + 1):
        pl.when(high - low == count)(functools.partial(body, count))


def attend(scale, first_tile, tiles, low, queries, keys, values, docs, across, before):
    block, width = queries.shape
    tile = HEAD_SIZE
    group = width // HEAD_SIZE
    most = (block + tile + KEY_TILE - 1) // KEY_TILE
    rows = lambda i: (first_tile + i, 0)
    whole = lambda i: (0, 0)
    in_specs = [
        SMEM,
        pl.BlockSpec((tile, width), rows),
        pl.BlockSpec(keys.shape, whole),
        pl.BlockSpec(values.shape, whole),
        pl.BlockSpec((tile, 1), rows),
        pl.BlockSpec(across.shape, whole),
    ]
    operands = [low, queries, keys, values, docs, across]
    aliases = {}
    if before is not None:
        in_specs.append(pl.BlockSpec(memory_space=pl.ANY))
        operands.append(before)
        aliases = {len(operands) - 1: 0}
    pairs = tiles * group * tile * 4 * KEY_TILE
    return pl.pallas_call(
        functools.partial(main_kernel, scale, first_tile),
        grid=(tiles,),
        out_shape=shape_of((block, width), bf16),
        in_specs=in_specs,
        out_specs=pl.BlockSpec((tile, width), rows),
        scratch_shapes=[
            pltpu.VMEM((tile, most * KEY_TILE), f32),
            pltpu.VMEM((group, tile, most * KEY_TILE), f32),
        ],
        input_output_aliases=aliases,
        compiler_params=params(),
        cost_estimate=cost(pairs * 6 * HEAD_SIZE, 2 * 2**20, pairs),
    )(*operands)


def to_heads(value):
    return lax.all_to_all(value, "head", split_axis=0, concat_axis=0, tiled=True)


def after(value, *others):
    return lax.optimization_barrier((value, *others))[0]


def local(
    queries, keys, values, doc_ids, sample_rows, owners, targets, in_proj, dec_gain, code_heads
):
    heads = lax.axis_size("head")
    contexts = lax.axis_size("ctx")
    head_number = lax.axis_index("head")
    ctx_number = lax.axis_index("ctx")
    frames = keys.shape[0]
    block = doc_ids.shape[0]
    samples = sample_rows.shape[0]
    per_head = samples // heads
    width = queries.shape[1] // heads
    group = width // HEAD_SIZE
    scale = math.log2(math.e) / math.sqrt(HEAD_SIZE)
    deep = in_proj.shape[1]
    books = targets.shape[1]

    packed = pl.pallas_call(
        functools.partial(pack_kernel, group),
        out_shape=shape_of((heads, 2 * frames + group * per_head, HEAD_SIZE), bf16),
        in_specs=[SMEM, ANY, ANY, ANY],
        out_specs=VMEM,
        scratch_shapes=[
            pltpu.VMEM(keys.shape, bf16),
            pltpu.VMEM(values.shape, bf16),
            pltpu.VMEM(queries.shape, bf16),
            pltpu.SemaphoreType.DMA((frames // 32 + 2,)),
        ],
        compiler_params=params(56),
        cost_estimate=cost(2 * per_head * frames * queries.shape[1], 2 * 2**20),
    )(sample_rows, keys, values, queries)
    own = to_heads(packed)

    ring = [(s, (s + 1) % contexts) for s in range(contexts)]
    half = heads // 2
    marked = doc_ids + 1
    told = jnp.where(ctx_number == contexts - 1, 0, marked).astype(bf16).reshape(heads, frames)
    first = own[:half, : 2 * frames].reshape(block, HEAD_SIZE)
    second = own[half:, : 2 * frames].reshape(block, HEAD_SIZE)
    second = jnp.concatenate([second, told, jnp.zeros_like(told)], axis=0)
    first = lax.ppermute(first, "ctx", ring)
    second = lax.ppermute(second, "ctx", ring)
    by_head = jnp.transpose(queries.reshape(frames, heads, width), (1, 0, 2))
    queries_here = to_heads(after(by_head, own)).reshape(block, width)

    docs = marked.astype(f32).reshape(heads, frames)
    spots = jnp.arange(block, dtype=jnp.int32)
    sample_docs = jnp.sum(
        jnp.where(sample_rows[:, None] == spots[None, :], marked[None, :], 0), axis=1
    )
    mine = jnp.stack([sample_docs, sample_rows + block], axis=1).astype(f32)
    mine = jnp.broadcast_to(
        mine.reshape(heads, 1, per_head, 2), (heads, group, per_head, 2)
    ).reshape(heads * group * per_head, 2)

    shares = pl.pallas_call(
        functools.partial(sample_kernel, scale),
        out_shape=shape_of((heads, samples, deep), bf16),
        in_specs=[VMEM] * 6,
        out_specs=VMEM,
        scratch_shapes=[pltpu.VMEM((samples * group, 2 * block), f32)],
        compiler_params=params(),
        cost_estimate=cost(
            4 * samples * group * 2 * block * HEAD_SIZE, 4 * 2**20, samples * group * 2 * block
        ),
    )(own, first, second, docs, mine, in_proj)

    all_keys, all_values, across, low = pl.pallas_call(
        unpack_kernel,
        out_shape=(
            shape_of((2 * block, HEAD_SIZE), bf16),
            shape_of((2 * block, 2 * HEAD_SIZE), bf16),
            shape_of((2 * heads, frames), f32),
            shape_of((block // HEAD_SIZE,), jnp.int32),
        ),
        in_specs=[VMEM] * 4 + [SMEM],
        out_specs=(VMEM, VMEM, VMEM, SMEM),
        compiler_params=params(),
        cost_estimate=cost(0, 3 * 2**20),
    )(after(own, shares), first, second, docs, marked[::HEAD_SIZE])

    parts = to_heads(after(shares, queries_here))
    tiles = block // HEAD_SIZE
    attended = attend(
        scale,
        0,
        tiles,
        low,
        queries_here,
        all_keys,
        all_values,
        marked.astype(f32)[:, None],
        across,
        None,
    )
    parts, attended = lax.optimization_barrier((parts, attended))

    codes_here = code_heads.shape[2]
    stats = pl.pallas_call(
        logits_kernel,
        out_shape=shape_of((heads, 8, 128), f32),
        in_specs=[VMEM] * 4,
        out_specs=VMEM,
        compiler_params=params(),
        cost_estimate=cost(4 * samples * deep * codes_here * books, code_heads.size * 2),
    )(parts, dec_gain[None, :], code_heads, targets - head_number * codes_here)
    all_stats = to_heads(stats)

    owner_ids = owners[:, 0]
    positions = jnp.arange(samples, dtype=jnp.int32)
    same = (owner_ids[None, :] == owner_ids[:, None]) & (positions[None, :] < positions[:, None])
    ranks = jnp.sum(same.astype(jnp.int32), axis=1)
    owner_pad = jnp.concatenate([owner_ids, jnp.full((128 - samples,), -1, jnp.int32)])
    slot_count = 2 * contexts
    owner_hit = (owner_pad[None, :] == jnp.arange(contexts)[:, None]).astype(f32)
    slots = jnp.concatenate([2 * ctx_number + ranks, jnp.full((128 - samples,), -1, jnp.int32)])
    slot_hit = (slots[:, None] == jnp.arange(slot_count)[None, :]).astype(f32)
    placed = pl.pallas_call(
        functools.partial(place_kernel, books),
        out_shape=shape_of((contexts, slot_count), f32),
        in_specs=[VMEM] * 3,
        out_specs=VMEM,
        compiler_params=params(),
        cost_estimate=cost(10**6, 10**5),
    )(all_stats, owner_hit, slot_hit)
    arrived = lax.all_to_all(placed, "ctx", split_axis=0, concat_axis=0, tiled=True)
    slot_loss = jnp.sum(arrived, axis=0, keepdims=True)
    return (attended, slot_loss)


def solution(mesh):
    in_specs = (
        P(("ctx", "head"), None),
        P(("ctx", "head"), None),
        P(("ctx", "head"), None),
        P("ctx"),
        P("ctx"),
        P("ctx", None),
        P("ctx", None),
        P("head", None),
        P(),
        P(None, None, "head"),
    )
    out_specs = (P("ctx", "head"), P("ctx", None))
    return jax.shard_map(local, mesh=mesh, in_specs=in_specs, out_specs=out_specs, check_vma=False)
```

time: 266 us -> 109 us (0.41)
  waiting for transfers between devices: 74.2 us -> 31.7 us
  blocking collectives: 59.9 us -> 22.6 us
  matrix products: 21.4 us -> 0 us
  other arithmetic: 23.1 us -> 1.87 us
  loops' own time: 16.9 us -> 0 us
  Pallas kernels: 0 us -> 15.6 us
  local copies, waits for them, and re-layouts: 21.7 us -> 7.91 us
  between operations: 14.2 us -> 0.78 us
  starting transfers between devices: 33.9 us -> 28 us
    psum x1 -> x0, waiting for transfers between devices: 46.7 us -> none  [local(): lax.psum(jnp.dot(arrived, in_proj, preferred_element_type=jnp.float32), '...]
    dot_general x20 -> x0, matrix products: 21.4 us -> none  [the longest x8 9.96 us: one_tile(): jnp.einsum('qgk,kd->qgd', rounded, head_values, preferred_element_type=jn...]
    another operation x1 -> x0, loops' own time: 16.9 us -> none  [local(): result = lax.map(one_tile, (head_queries, offsets))]
    pallas_call x0 -> x6, Pallas kernels: none -> 15.6 us  [the longest x1 6.99 us: attend(): pl.pallas_call(functools.partial(main_kernel, scale, first_tile), grid=(t...]
    pmax x1 -> x0, blocking collectives: 14 us -> none  [local(): row_top = lax.pmax(local_top, 'head')]
    psum x1 -> x0, blocking collectives: 13.8 us -> none  [local(): lax.psum((jnp.sum(jnp.exp(logits - row_top[..., None]), axis=-1), target_...]
    reduce_sum x12 -> x3, other arithmetic: 11.3 us -> 1.55 us  [the longest x1 0.77 us: local(): ranks = jnp.sum(same.astype(jnp.int32), axis=1)]
    all_to_all x1, blocking collectives: 32.1 us -> 22.6 us  [local(): lax.all_to_all(placed, 'ctx', split_axis=0, concat_axis=0, tiled=True)]
  transfers between devices with their start and end apart: 8 -> 6, of which waited for: 7 -> 5; matrix products, arithmetic and copies ran while one was open for 4% -> 5% of each run, Pallas kernels for 0% -> 10%
where the time goes in v1:
time: 109 us; the launch traced here: 108 us
  waiting for transfers between devices  31.7 us (29%)
  starting transfers between devices  28 us (26%)
  blocking collectives  22.6 us (21%)
  Pallas kernels  15.6 us (14%)
  local copies, waits for them, and re-layouts  7.91 us (7%)
  other arithmetic  1.87 us (2%)
    all_to_all x4, starting transfers between devices, to_heads(): lax.all_to_all(value, 'head', split_axis=0, concat_axis=0, tiled=True)  24.2 us
    all_to_all x1, blocking collectives, local(): lax.all_to_all(placed, 'ctx', split_axis=0, concat_axis=0, tiled=True)  22.6 us
    all_to_all x4, waiting for transfers between devices, to_heads(): lax.all_to_all(value, 'head', split_axis=0, concat_axis=0, tiled=True)  18.7 us
    ppermute x1, waiting for transfers between devices, local(): first = lax.ppermute(first, 'ctx', ring)  7.3 us
    pallas_call x1, Pallas kernels, attend(): pl.pallas_call(functools.partial(main_kernel, scale, first_tile), grid=(t...  6.99 us
    ppermute x1, waiting for transfers between devices, local(): second = lax.ppermute(second, 'ctx', ring)  5.7 us
    unnamed x25, local copies, waits for them, and re-layouts  4.06 us
    pallas_call x1, Pallas kernels, local(): pl.pallas_call(functools.partial(pack_kernel, group), out_shape=shape_of(...  3.13 us
  transfers between devices with their start and end apart: 6, of which 5 were waited for; matrix products, arithmetic and copies ran while one was open for 5% of the time, Pallas kernels for 10%

profile of v1, /device:TPU:1, one launch (start us, length us, event | category | flops | bytes accessed | tf_op | source)
XLA Modules:
  0.0 108.5 jit_solution(11197637244205176612)
XLA Ops:
  0.6 3.1 %shard_map.113 = bf16[8,288,128]{2,1,0:T(8,128)(2,1)} custom-call(s32[64]{0:T(128)} %rows_ref.1, bf16[128,1024]{1,0:T(8,128)(2,1)} %keys_hbm.1, bf16[128,1024]{1,0:T(8,128)(2,1)} %values_hbm.1, bf16[128,4096]{1,0:T(8,128)(2,1)} %queries_hbm.1), custom_call_target="tpu_custom_call" | custom-call | flops 8388608 | bytes 2097152 | tf_op jit(solution)/shard_map/pallas_call | solution.py:322
  3.8 10.5 %all-to-all-start = ((bf16[8,288,128]{2,1,0:T(8,128)(2,1)}), bf16[8,288,128]{2,1,0:T(8,128)(2,1)S(1)}, u32[]{:S(2)}, u32[]{:S(2)}) async-start(bf16[8,288,128]{2,1,0:T(8,128)(2,1)} %shard_map.113), calls=%async_computation | async-start | bytes 1179648 | tf_op jit(solution)/shard_map/all_to_all | solution.py:298
  14.2 1.1 copy.37
  15.4 0.6 copy-done.8
  16.0 8.4 %all-to-all-done.own_ref = bf16[8,288,128]{2,1,0:T(8,128)(2,1)S(1)} async-done(((bf16[8,288,128]{2,1,0:T(8,128)(2,1)}), bf16[8,288,128]{2,1,0:T(8,128)(2,1)S(1)}, u32[]{:S(2)}, u32[]{:S(2)}) %all-to-all-start) | async-done | bytes 589856 | tf_op jit(solution)/shard_map/all_to_all | solution.py:298
  24.4 4.3 %all-to-all-start.1 = ((bf16[8,128,512]{2,1,0:T(8,128)(2,1)}), bf16[8,128,512]{2,1,0:T(8,128)(2,1)S(1)}, u32[]{:S(2)}, u32[]{:S(2)}) async-start(bf16[8,128,512]{2,1,0:T(8,128)(2,1)} %bitcast.27), calls=%async_computation.1 | async-start | bytes 2097152 | tf_op jit(solution)/shard_map/all_to_all | solution.py:298
  28.8 0.7 fusion.5
  29.5 1.9 %collective-permute-start = (bf16[1024,128]{1,0:T(8,128)(2,1)}, bf16[1024,128]{1,0:T(8,128)(2,1)S(1)}, u32[]{:S(2)}, u32[]{:S(2)}) collective-permute-start(bf16[1024,128]{1,0:T(8,128)(2,1)} %bitcast), channel_id=1, source_target_pairs={{0,8},{8,16},{16,24},{24,32},{32,40},{40,48},{48,56},{56,64},{64,7... | collective-permute-start | bytes 786440 | tf_op jit(solution)/shard_map/ppermute | solution.py:345
  31.4 0.2 maximum_maximum_fusion
  31.6 1.9 %collective-permute-start.1 = (bf16[1040,128]{1,0:T(8,128)(2,1)S(1)}, bf16[1040,128]{1,0:T(8,128)(2,1)S(1)}, u32[]{:S(2)}, u32[]{:S(2)}) collective-permute-start(bf16[1040,128]{1,0:T(8,128)(2,1)S(1)} %maximum_maximum_fusion), channel_id=1, source_target_pairs={{0,8},{8,16},{16,24},{24,32},{32,40},{40,48},{48,56},{56,64},{64,7... | collective-permute-start | bytes 798728 | tf_op jit(solution)/shard_map/ppermute | solution.py:346
  33.6 0.2 select_reduce_fusion
  34.0 0.1 copy.29
  34.1 1.1 copy.31.docs_ref
  35.2 0.8 copy.32
  36.0 0.7 copy-done.10
  36.6 0.5 concatenate.14
  37.1 0.8 convert_reduce_fusion
  37.9 7.3 %collective-permute-done.first_ref = bf16[1024,128]{1,0:T(8,128)(2,1)S(1)} collective-permute-done((bf16[1024,128]{1,0:T(8,128)(2,1)}, bf16[1024,128]{1,0:T(8,128)(2,1)S(1)}, u32[]{:S(2)}, u32[]{:S(2)}) %collective-permute-start) | collective-permute-done | bytes 262176 | tf_op jit(solution)/shard_map/ppermute | solution.py:345
  45.2 5.7 %collective-permute-done.1.second_ref = bf16[1040,128]{1,0:T(8,128)(2,1)S(1)} collective-permute-done((bf16[1040,128]{1,0:T(8,128)(2,1)S(1)}, bf16[1040,128]{1,0:T(8,128)(2,1)S(1)}, u32[]{:S(2)}, u32[]{:S(2)}) %collective-permute-start.1) | collective-permute-done | bytes 266272 | tf_op jit(solution)/shard_map/ppermute | solution.py:346
  50.9 2.6 %shard_map.114 = bf16[8,64,1024]{2,1,0:T(8,128)(2,1)} custom-call(bf16[8,288,128]{2,1,0:T(8,128)(2,1)S(1)} %all-to-all-done.own_ref, bf16[1024,128]{1,0:T(8,128)(2,1)S(1)} %collective-permute-done.first_ref, bf16[1040,128]{1,0:T(8,128)(2,1)S(1)} %collective-permute-done.1.second_ref, f32[8,128]{1,0:T(8,128)S(1)} %get-tuple-element.24.docs_ref, ...), custom_call_target="tpu_custom_call" | custom-call | flops 268435456 | bytes 4194304 | tf_op jit(solution)/shard_map/pallas_call | solution.py:360
  53.5 1.0 copy-done.2
  54.5 5.2 %all-to-all-start.2 = ((bf16[8,64,1024]{2,1,0:T(8,128)(2,1)}), bf16[8,64,1024]{2,1,0:T(8,128)(2,1)S(1)}, u32[]{:S(2)}, u32[]{:S(2)}) async-start(bf16[8,64,1024]{2,1,0:T(8,128)(2,1)} %shard_map.114), calls=%async_computation.2 | async-start | bytes 2097152 | tf_op jit(solution)/shard_map/all_to_all | solution.py:298
  59.8 1.4 %shard_map.115 = (bf16[2048,128]{1,0:T(8,128)(2,1)S(1)}, bf16[2048,256]{1,0:T(8,128)(2,1)S(1)}, f32[16,128]{1,0:T(8,128)S(1)}, s32[8]{0:T(128)S(1)}) custom-call(bf16[8,288,128]{2,1,0:T(8,128)(2,1)S(1)} %all-to-all-done.own_ref, bf16[1024,128]{1,0:T(8,128)(2,1)S(1)} %collective-permute-done.first_ref, ...), custom_call_target="tpu_custom_call" | custom-call | bytes 3145728 | tf_op jit(solution)/shard_map/pallas_call | solution.py:372
  61.2 1.0 copy-done.4
  62.2 7.0 %shard_map.116 = bf16[1024,512]{1,0:T(8,128)(2,1)} custom-call(s32[8]{0:T(128)S(1)} %get-tuple-element.14.low_ref, bf16[1024,512]{1,0:T(8,128)(2,1)S(1)} %bitcast.22, bf16[2048,128]{1,0:T(8,128)(2,1)S(1)} %get-tuple-element.15.keys_ref, bf16[2048,256]{1,0:T(8,128)(2,1)S(1)} %get-tuple-element.16.values_ref, f32[1024,1]{1,0:T(8,128)S(1)} %copy-done.4, ...), custom_call_target="tpu_custom_call" | custom-call | flops 3221225472 | bytes 2097152 | tf_op jit(solution)/shard_map/pallas_call | solution.py:281
  69.2 5.5 %all-to-all-done.2.parts_ref = bf16[8,64,1024]{2,1,0:T(8,128)(2,1)S(1)} async-done(((bf16[8,64,1024]{2,1,0:T(8,128)(2,1)}), bf16[8,64,1024]{2,1,0:T(8,128)(2,1)S(1)}, u32[]{:S(2)}, u32[]{:S(2)}) %all-to-all-start.2) | async-done | bytes 1048608 | tf_op jit(solution)/shard_map/all_to_all | solution.py:298
  74.7 1.3 %shard_map.117 = f32[8,8,128]{2,1,0:T(8,128)} custom-call(bf16[8,64,1024]{2,1,0:T(8,128)(2,1)S(1)} %all-to-all-done.2.parts_ref, f32[1,1024]{1,0:T(1,128)S(1)} %bitcast.25, bf16[2,1024,256]{2,1,0:T(8,128)(2,1)S(1)} %copy-done.1, s32[64,2]{1,0:T(8,128)S(1)} %broadcast_subtract_fusion.targets_ref), custom_call_target="tpu_custom_call" | custom-call | flops 134217728 | bytes 1048576 | tf_op jit(solution)/shard_map/pallas_call | solution.py:403
  76.1 4.2 %all-to-all-start.3 = ((f32[8,8,128]{2,1,0:T(8,128)}), f32[8,8,128]{2,1,0:T(8,128)S(1)}, u32[]{:S(2)}, u32[]{:S(2)}) async-start(f32[8,8,128]{2,1,0:T(8,128)} %shard_map.117), calls=%async_computation.3 | async-start | bytes 65536 | tf_op jit(solution)/shard_map/all_to_all | solution.py:298
  80.3 4.7 %all-to-all-done.3.stats_ref = f32[8,8,128]{2,1,0:T(8,128)S(1)} async-done(((f32[8,8,128]{2,1,0:T(8,128)}), f32[8,8,128]{2,1,0:T(8,128)S(1)}, u32[]{:S(2)}, u32[]{:S(2)}) %all-to-all-start.3) | async-done | bytes 32800 | tf_op jit(solution)/shard_map/all_to_all | solution.py:298
  85.0 0.2 shard_map.118
  85.2 22.6 %all_to_all.29 = f32[64,1,128]{2,1,0:T(1,128)S(1)} all-to-all(f32[64,1,128]{2,1,0:T(1,128)S(1)} %bitcast.24), channel_id=1, replica_groups=mesh['ctx'=64,'head'=8] {'ctx'}, dimensions={0} | all-to-all | bytes 65536 | tf_op jit(solution)/shard_map/all_to_all | solution.py:430
  107.9 0.6 reduce_sum.29
  (35 shorter events, 0.5 us)
Async XLA Ops:
  3.8 10.5 %copy-start.6 = (bf16[128,4096]{1,0:T(8,128)(2,1)S(1)}, bf16[128,4096]{1,0:T(8,128)(2,1)}, u32[]{:S(2)}) copy-start(bf16[128,4096]{1,0:T(8,128)(2,1)} %queries_hbm.1) | copy-start | bytes 3145732
  3.8 20.7 %all-to-all-start = ((bf16[8,288,128]{2,1,0:T(8,128)(2,1)}), bf16[8,288,128]{2,1,0:T(8,128)(2,1)S(1)}, u32[]{:S(2)}, u32[]{:S(2)}) async-start(bf16[8,288,128]{2,1,0:T(8,128)(2,1)} %shard_map.113), calls=%async_computation | async-start | bytes 1179648 | tf_op jit(solution)/shard_map/all_to_all | solution.py:298
  15.3 0.7 copy-start.7
  15.3 0.7 copy-start.8
  24.4 29.1 %all-to-all-start.1 = ((bf16[8,128,512]{2,1,0:T(8,128)(2,1)}), bf16[8,128,512]{2,1,0:T(8,128)(2,1)S(1)}, u32[]{:S(2)}, u32[]{:S(2)}) async-start(bf16[8,128,512]{2,1,0:T(8,128)(2,1)} %bitcast.27), calls=%async_computation.1 | async-start | bytes 2097152 | tf_op jit(solution)/shard_map/all_to_all | solution.py:298
  28.8 22.2 %copy-start = (bf16[512,1024]{1,0:T(8,128)(2,1)S(1)}, bf16[512,1024]{1,0:T(8,128)(2,1)}, u32[]{:S(2)}) copy-start(bf16[512,1024]{1,0:T(8,128)(2,1)} %proj_ref.1) | copy-start | bytes 3145732
  29.5 15.7 %collective-permute-start = (bf16[1024,128]{1,0:T(8,128)(2,1)}, bf16[1024,128]{1,0:T(8,128)(2,1)S(1)}, u32[]{:S(2)}, u32[]{:S(2)}) collective-permute-start(bf16[1024,128]{1,0:T(8,128)(2,1)} %bitcast), channel_id=1, source_target_pairs={{0,8},{8,16},{16,24},{24,32},{32,40},{40,48},{48,56},{56,64},{64,7... | collective-permute-start | bytes 786440 | tf_op jit(solution)/shard_map/ppermute | solution.py:345
  31.6 19.3 %collective-permute-start.1 = (bf16[1040,128]{1,0:T(8,128)(2,1)S(1)}, bf16[1040,128]{1,0:T(8,128)(2,1)S(1)}, u32[]{:S(2)}, u32[]{:S(2)}) collective-permute-start(bf16[1040,128]{1,0:T(8,128)(2,1)S(1)} %maximum_maximum_fusion), channel_id=1, source_target_pairs={{0,8},{8,16},{16,24},{24,32},{32,40},{40,48},{48,56},{56,64},{64,7... | collective-permute-start | bytes 798728 | tf_op jit(solution)/shard_map/ppermute | solution.py:346
  36.0 0.7 copy-start.10
  53.5 1.0 copy-start.2
  53.5 6.1 %copy-start.11 = (s32[64]{0:T(128)S(1)}, s32[64]{0:T(128)}, u32[]{:S(2)}) copy-start(s32[64]{0:T(128)} %convert_reduce_fusion) | copy-start | bytes 772
  54.5 20.3 %all-to-all-start.2 = ((bf16[8,64,1024]{2,1,0:T(8,128)(2,1)}), bf16[8,64,1024]{2,1,0:T(8,128)(2,1)S(1)}, u32[]{:S(2)}, u32[]{:S(2)}) async-start(bf16[8,64,1024]{2,1,0:T(8,128)(2,1)} %shard_map.114), calls=%async_computation.2 | async-start | bytes 2097152 | tf_op jit(solution)/shard_map/all_to_all | solution.py:298
  59.7 1.5 %copy-start.3 = (bf16[8,128,512]{2,1,0:T(8,128)(2,1)S(1)}, bf16[8,128,512]{2,1,0:T(8,128)(2,1)}, u32[]{:S(2)}) copy-start(bf16[8,128,512]{2,1,0:T(8,128)(2,1)} %copy-done.2) | copy-start | bytes 3145732
  61.2 1.0 copy-start.4
  62.2 12.5 %copy-start.1 = (bf16[2,1024,256]{2,1,0:T(8,128)(2,1)S(1)}, bf16[2,1024,256]{2,1,0:T(8,128)(2,1)}, u32[]{:S(2)}) copy-start(bf16[2,1024,256]{2,1,0:T(8,128)(2,1)} %codes_ref.1) | copy-start | bytes 3145732
  62.2 12.5 %copy-start.5 = (f32[1024]{0:T(1024)S(1)}, f32[1024]{0:T(1024)}, u32[]{:S(2)}) copy-start(f32[1024]{0:T(1024)} %param.18) | copy-start | bytes 12292
  76.0 4.2 %copy-start.9 = (s32[128]{0:T(128)S(1)}, s32[128]{0:T(128)}, u32[]{:S(2)}) copy-start(s32[128]{0:T(128)} %concatenate.14) | copy-start | bytes 1540
  76.1 9.0 %all-to-all-start.3 = ((f32[8,8,128]{2,1,0:T(8,128)}), f32[8,8,128]{2,1,0:T(8,128)S(1)}, u32[]{:S(2)}, u32[]{:S(2)}) async-start(f32[8,8,128]{2,1,0:T(8,128)} %shard_map.117), calls=%async_computation.3 | async-start | bytes 65536 | tf_op jit(solution)/shard_map/all_to_all | solution.py:298

commit v2 on v1

v2 whole, which is shorter than its diff:
```python
import functools
import math

import jax
import jax.numpy as jnp
from jax import lax
from jax.experimental import pallas as pl
from jax.experimental.pallas import tpu as pltpu
from jax.sharding import PartitionSpec as P

HEAD_SIZE = 128
KEY_TILE = 256
CUT = 4
QUERY_TILE = 256
MASKED = -1e30
bf16 = jnp.bfloat16
f32 = jnp.float32
VMEM = pl.BlockSpec(memory_space=pltpu.VMEM)
SMEM = pl.BlockSpec(memory_space=pltpu.SMEM)
ANY = pl.BlockSpec(memory_space=pl.ANY)


def params(mib=14):
    return pltpu.CompilerParams(vmem_limit_bytes=mib * 2**20)


def cost(flops, moved, exps=0):
    return pl.CostEstimate(flops=flops, bytes_accessed=moved, transcendentals=exps)


def shape_of(shape, dtype):
    return jax.ShapeDtypeStruct(shape, dtype)


def pack_kernel(group, rows_ref, keys_hbm, values_hbm, queries_hbm, out_ref, queries_ref, sems):
    heads = out_ref.shape[0]
    frames = queries_ref.shape[0]
    per_head = rows_ref.shape[0] // heads
    copies = []
    for which, ref in enumerate((keys_hbm, values_hbm)):
        for g in range(heads):
            copies.append(
                pltpu.make_async_copy(
                    ref.at[:, pl.ds(g * HEAD_SIZE, HEAD_SIZE)],
                    out_ref.at[g, pl.ds(which * frames, frames), :],
                    sems.at[which * heads + g],
                )
            )
    pieces = []
    for p in range(4):
        span = pl.ds(p * (frames // 4), frames // 4)
        pieces.append(
            pltpu.make_async_copy(
                queries_hbm.at[span], queries_ref.at[span], sems.at[2 * heads + p]
            )
        )
    for copy in pieces + copies:
        copy.start()
    me = lax.axis_index("head")
    row = lax.broadcasted_iota(jnp.int32, (per_head, frames), 0)
    lane = lax.broadcasted_iota(jnp.int32, (per_head, frames), 1)
    wanted = jnp.full((per_head, frames), -1, jnp.int32)
    for i in range(per_head):
        wanted = jnp.where(row == i, rows_ref[me * per_head + i] - me * frames, wanted)
    chosen = jnp.where(lane == wanted, 1.0, 0.0).astype(bf16)
    for copy in pieces:
        copy.wait()
    picked = jnp.dot(chosen, queries_ref[...], preferred_element_type=f32)
    for g in range(heads):
        parts = [
            picked[:, (g * group + j) * HEAD_SIZE : (g * group + j + 1) * HEAD_SIZE]
            for j in range(group)
        ]
        out_ref[g, pl.ds(2 * frames, group * per_head), :] = jnp.concatenate(parts, axis=0).astype(
            bf16
        )
    for copy in copies:
        copy.wait()


def turned(row):
    return jnp.transpose(jnp.broadcast_to(row, (128, 128)))


def prep_kernel(
    group, rows_ref, ids_ref, owners_ref, targets_ref, docs_ref, told_ref, mine_ref, info_ref
):
    heads, frames = ids_ref.shape
    samples = rows_ref.shape[0]
    per_head = samples // heads
    docs = (ids_ref[...] + 1).astype(f32)
    docs_ref[...] = docs
    last = lax.axis_index("ctx") == lax.axis_size("ctx") - 1
    told_ref[...] = jnp.where(last, 0.0, docs)
    row = lax.broadcasted_iota(jnp.int32, (per_head, frames), 0)
    lane = lax.broadcasted_iota(jnp.int32, (per_head, frames), 1)
    for s in range(heads):
        place = jnp.zeros((per_head, frames), jnp.int32)
        for i in range(per_head):
            place = jnp.where(row == i, rows_ref[s * per_head + i] - s * frames, place)
        doc = jnp.sum(jnp.where(lane == place, docs[s : s + 1], 0.0), axis=1, keepdims=True)
        spot = ((heads + s) * frames + place).astype(f32)
        both = jnp.where(lane == 0, doc, spot)
        for j in range(group):
            mine_ref[pl.ds((s * group + j) * per_head, per_head), :] = both
    info_ref[...] = jnp.full(info_ref.shape, -1.0, f32)
    info_ref[0:1, 0:samples] = owners_ref[...].astype(f32)
    info_ref[2 : 2 + targets_ref.shape[0], 0:samples] = targets_ref[...].astype(f32)
    across = jnp.broadcast_to(info_ref[0:1, :], (128, 128))
    row = lax.broadcasted_iota(jnp.int32, (128, 128), 0)
    lane = lax.broadcasted_iota(jnp.int32, (128, 128), 1)
    same = (jnp.transpose(across) == across) & (row < lane)
    rank = jnp.sum(jnp.where(same, 1.0, 0.0), axis=0, keepdims=True)
    info_ref[1:2, :] = rank + (2 * lax.axis_index("ctx")).astype(f32)


def block_rows(s, own_ref, first_ref, second_ref, frames, which):
    heads = own_ref.shape[0]
    half = heads // 2
    if s >= heads:
        return own_ref[s - heads, pl.ds(which * frames, frames), :]
    ref, at = (first_ref, s) if s < half else (second_ref, s - half)
    return ref[pl.ds((2 * at + which) * frames, frames), :]


def unpack_kernel(
    own_ref, first_ref, second_ref, before_ref, docs_ref, keys_ref, values_ref, all_docs_ref, low_ref
):
    heads = own_ref.shape[0]
    frames = docs_ref.shape[1]
    for s in range(2 * heads):
        rows = pl.ds(s * frames, frames)
        keys_ref[rows, :] = block_rows(s, own_ref, first_ref, second_ref, frames, 0)
        values_ref[rows, :] = block_rows(s, own_ref, first_ref, second_ref, frames, 1)
    docs = jnp.concatenate([before_ref[...], docs_ref[...]], axis=0)
    all_docs_ref[...] = docs
    for t in range(low_ref.shape[0]):
        below = jnp.where(docs < docs_ref[t : t + 1, 0:1], 1.0, 0.0)
        low_ref[t] = jnp.sum(below).astype(jnp.int32) // KEY_TILE


def sample_kernel(
    scale,
    own_ref,
    first_ref,
    second_ref,
    before_ref,
    docs_ref,
    mine_ref,
    proj_ref,
    keep_ref,
    send_ref,
    scores_ref,
):
    heads = own_ref.shape[0]
    frames = docs_ref.shape[1]
    extra = own_ref.shape[1] - 2 * frames
    group = proj_ref.shape[0] // HEAD_SIZE
    per_head = extra // group
    rows = heads * extra
    tile = 2 * frames
    queries = own_ref[:, pl.ds(2 * frames, extra), :].reshape(rows, HEAD_SIZE)
    docs = jnp.concatenate([before_ref[...], docs_ref[...]], axis=0)
    my_doc = jnp.broadcast_to(mine_ref[:, 0:1], (rows, tile))
    my_place = jnp.broadcast_to(mine_ref[:, 1:2], (rows, tile))
    lane = lax.broadcasted_iota(jnp.int32, (rows, tile), 1).astype(f32)
    highest = jnp.full((rows, HEAD_SIZE), MASKED, f32)
    for s in range(0, 2 * heads, 2):
        key_tile = jnp.concatenate(
            [block_rows(s + i, own_ref, first_ref, second_ref, frames, 0) for i in range(2)], axis=0
        )
        scores = lax.dot_general(
            queries, key_tile, (((1,), (1,)), ((), ())), preferred_element_type=f32
        )
        tile_docs = jnp.concatenate([docs[s : s + 1], docs[s + 1 : s + 2]], axis=1)
        seen = (tile_docs == my_doc) & (lane <= my_place - s * frames)
        scores = jnp.where(seen, scores * scale, MASKED)
        start = s * frames
        scores_ref[:, start : start + tile] = scores
        for part in range(tile // HEAD_SIZE):
            highest = jnp.maximum(highest, scores[:, part * HEAD_SIZE : (part + 1) * HEAD_SIZE])
    top = jnp.max(highest, axis=1, keepdims=True)
    total = jnp.zeros((rows, HEAD_SIZE), f32)
    mixed = jnp.zeros((rows, HEAD_SIZE), f32)
    for s in range(0, 2 * heads, 2):
        value_tile = jnp.concatenate(
            [block_rows(s + i, own_ref, first_ref, second_ref, frames, 1) for i in range(2)], axis=0
        )
        start = s * frames
        weights = jnp.exp2(scores_ref[:, start : start + tile] - top)
        for part in range(tile // HEAD_SIZE):
            total = total + weights[:, part * HEAD_SIZE : (part + 1) * HEAD_SIZE]
        mixed = mixed + jnp.dot(weights.astype(bf16), value_tile, preferred_element_type=f32)
    attended = mixed / jnp.sum(total, axis=1, keepdims=True)
    by_group = attended.reshape(heads, group, per_head, HEAD_SIZE)
    state = jnp.zeros((heads * per_head, proj_ref.shape[1]), f32)
    for j in range(group):
        part = by_group[:, j].reshape(heads * per_head, HEAD_SIZE).astype(bf16)
        state = state + jnp.dot(
            part, proj_ref[pl.ds(j * HEAD_SIZE, HEAD_SIZE), :], preferred_element_type=f32
        )
    rows = state.shape[0] // 2
    odd = lax.rem(lax.axis_index("head"), 2) == 1
    keep_ref[...] = jnp.where(odd, state[rows:], state[:rows])
    send_ref[...] = jnp.where(odd, state[:rows], state[rows:]).astype(bf16)


def pair_kernel(keep_ref, came_ref, out_ref):
    state = (keep_ref[...] + came_ref[...].astype(f32)).astype(bf16)
    for d in range(out_ref.shape[0]):
        out_ref[d] = state


def logits_kernel(parts_ref, gain_ref, codes_ref, other_ref, info_ref, out_ref):
    count, samples, width = parts_ref.shape
    books, _, codes = codes_ref.shape
    me = lax.axis_index("head")
    odd = lax.rem(me, 2) == 1
    other = jnp.where(odd, me - 1, me + 1)
    state = parts_ref[0].astype(f32)
    for s in range(1, count):
        state = state + parts_ref[s].astype(f32)
    square = jnp.sum(state * state, axis=1, keepdims=True)
    normed = (state * lax.rsqrt(square / width + 1e-06) * gain_ref[...]).astype(bf16)
    lane = lax.broadcasted_iota(jnp.int32, (samples, 128), 1)
    code = lax.broadcasted_iota(jnp.int32, (samples, codes), 1).astype(f32)
    stats = jnp.zeros((samples, 128), f32)
    for b in range(books):
        first = jnp.dot(normed, codes_ref[b], preferred_element_type=f32)
        second = jnp.dot(normed, other_ref[b], preferred_element_type=f32)
        top = jnp.max(jnp.maximum(first, second), axis=1, keepdims=True)
        mass = jnp.sum(jnp.exp(first - top) + jnp.exp(second - top), axis=1, keepdims=True)
        column = turned(info_ref[2 + b : 3 + b, :])
        wanted = jnp.where(odd, column[samples : 2 * samples], column[:samples])[:, 0:1]
        hit = jnp.where(code == wanted - (me * codes).astype(f32), first, 0.0)
        hit = hit + jnp.where(code == wanted - (other * codes).astype(f32), second, 0.0)
        target = jnp.sum(hit, axis=1, keepdims=True)
        for k, figure in enumerate((top, mass, target)):
            stats = jnp.where(lane == 3 * b + k, figure, stats)
    none = jnp.zeros((samples, 128), f32)
    padded = jnp.concatenate(
        [jnp.where(odd, none, stats), jnp.where(odd, stats, none), none, none], axis=0
    )
    across = jnp.transpose(padded)[:8]
    for d in range(out_ref.shape[0]):
        out_ref[d] = across


def place_kernel(books, samples, stats_ref, info_ref, out_ref):
    heads = stats_ref.shape[0]
    losses = []
    for core in range(2):
        loss = jnp.zeros((1, 128), f32)
        for b in range(books):
            tops = [stats_ref[s, 3 * b : 3 * b + 1, :] for s in range(core, heads, 2)]
            top = functools.reduce(jnp.maximum, tops)
            mass = jnp.zeros((1, 128), f32)
            target = jnp.zeros((1, 128), f32)
            for i, s in enumerate(range(core, heads, 2)):
                mass = mass + stats_ref[s, 3 * b + 1 : 3 * b + 2, :] * jnp.exp(tops[i] - top)
                target = target + stats_ref[s, 3 * b + 2 : 3 * b + 3, :]
            loss = loss + (jnp.log(mass) + top - target)
        losses.append(loss * (1.0 / books))
    lane = lax.broadcasted_iota(jnp.int32, (1, 128), 1)
    loss = jnp.where(lane < samples // 2, losses[0], losses[1])
    contexts, slots = out_ref.shape
    owner = lax.broadcasted_iota(jnp.int32, (contexts, 128), 0).astype(f32)
    spread = jnp.where(info_ref[0:1, :] == owner, loss, 0.0)
    column = lax.broadcasted_iota(jnp.int32, (128, 128), 1).astype(f32)
    column = jnp.where(turned(info_ref[1:2, :]) == column, 1.0, 0.0)[:, :slots]
    out_ref[...] = jnp.dot(
        spread, column, preferred_element_type=f32, precision=lax.Precision.HIGHEST
    )


def main_kernel(scale, first_tile, low_ref, queries_ref, keys_ref, values_ref, across_ref, *refs):
    out_ref, bias_ref, scores_ref = refs[-3:]
    tile, width = queries_ref.shape
    group = width // HEAD_SIZE
    parts = tile // HEAD_SIZE
    block = keys_ref.shape[0] // 2
    number = first_tile + pl.program_id(0)
    start = block + number * tile
    low = low_ref[number * parts]
    high = (start + tile + KEY_TILE - 1) // KEY_TILE
    halves = KEY_TILE // HEAD_SIZE
    units = [(j, r) for j in range(group) for r in range(parts)]

    def body(count):
        base = pl.multiple_of(low * KEY_TILE, KEY_TILE)
        ahead = lax.broadcasted_iota(jnp.int32, (HEAD_SIZE, HEAD_SIZE), 0) - lax.broadcasted_iota(
            jnp.int32, (HEAD_SIZE, HEAD_SIZE), 1
        )
        for r in range(parts):
            row = (block + number * tile) // HEAD_SIZE + r
            my_doc = turned(across_ref[pl.ds(row, 1), :])
            for k in range(count * halves):
                doc = across_ref[pl.ds(low * halves + k, 1), :]
                seen = (doc == my_doc) & (ahead >= base + k * HEAD_SIZE - start - r * HEAD_SIZE)
                bias_ref[r, :, k * HEAD_SIZE : (k + 1) * HEAD_SIZE] = jnp.where(seen, 0.0, MASKED)
        tops = []
        for u, (j, r) in enumerate(units):
            queries = queries_ref[r * HEAD_SIZE : (r + 1) * HEAD_SIZE, j * HEAD_SIZE : (j + 1) * HEAD_SIZE]
            highest = None
            for k in range(count):
                span = slice(k * KEY_TILE, (k + 1) * KEY_TILE)
                key_tile = keys_ref[pl.ds(base + k * KEY_TILE, KEY_TILE), :]
                scores = lax.dot_general(
                    queries, key_tile, (((1,), (1,)), ((), ())), preferred_element_type=f32
                )
                scores = scores * scale + bias_ref[r, :, span]
                scores_ref[u, :, span] = scores
                most = jnp.maximum(scores[:, :HEAD_SIZE], scores[:, HEAD_SIZE:])
                highest = most if highest is None else jnp.maximum(highest, most)
            tops.append(jnp.max(highest, axis=1, keepdims=True))
        one = jnp.ones((count * KEY_TILE, HEAD_SIZE), bf16)
        value_rows = jnp.concatenate([values_ref[pl.ds(base, count * KEY_TILE), :], one], axis=1)
        for u, (j, r) in enumerate(units):
            weights = jnp.concatenate(
                [
                    jnp.exp2(scores_ref[u, :, k * KEY_TILE : (k + 1) * KEY_TILE] - tops[u]).astype(bf16)
                    for k in range(count)
                ],
                axis=1,
            )
            mixed = jnp.dot(weights, value_rows, preferred_element_type=f32)
            out_ref[r * HEAD_SIZE : (r + 1) * HEAD_SIZE, j * HEAD_SIZE : (j + 1) * HEAD_SIZE] = (
                mixed[:, :HEAD_SIZE] / mixed[:, HEAD_SIZE:]
            ).astype(bf16)

    most = scores_ref.shape[2] // KEY_TILE
    for count in range(1, most + 1):
        pl.when(high - low == count)(functools.partial(body, count))


def attend(scale, first_tile, tiles, low, queries, keys, values, across, before):
    block, width = queries.shape
    tile = QUERY_TILE
    first_tile, tiles = first_tile * HEAD_SIZE // tile, tiles * HEAD_SIZE // tile
    group = width // HEAD_SIZE
    most = (block + tile + KEY_TILE - 1) // KEY_TILE
    rows = lambda i: (first_tile + i, 0)
    whole = lambda i: (0, 0)
    in_specs = [
        SMEM,
        pl.BlockSpec((tile, width), rows),
        pl.BlockSpec(keys.shape, whole),
        pl.BlockSpec(values.shape, whole),
        pl.BlockSpec(across.shape, whole),
    ]
    operands = [low, queries, keys, values, across]
    aliases = {}
    if before is not None:
        in_specs.append(pl.BlockSpec(memory_space=pl.ANY))
        operands.append(before)
        aliases = {len(operands) - 1: 0}
    pairs = tiles * group * tile * 4 * KEY_TILE
    return pl.pallas_call(
        functools.partial(main_kernel, scale, first_tile),
        grid=(tiles,),
        out_shape=shape_of((block, width), bf16),
        in_specs=in_specs,
        out_specs=pl.BlockSpec((tile, width), rows),
        scratch_shapes=[
            pltpu.VMEM((tile // HEAD_SIZE, HEAD_SIZE, most * KEY_TILE), f32),
            pltpu.VMEM((group * tile // HEAD_SIZE, HEAD_SIZE, most * KEY_TILE), f32),
        ],
        input_output_aliases=aliases,
        compiler_params=params(),
        cost_estimate=cost(pairs * 6 * HEAD_SIZE, 2 * 2**20, pairs),
    )(*operands)


def to_heads(value):
    return lax.all_to_all(value, "head", split_axis=0, concat_axis=0, tiled=True)


def after(value, *others):
    return lax.optimization_barrier((value, *others))[0]


def local(
    queries, keys, values, doc_ids, sample_rows, owners, targets, in_proj, dec_gain, code_heads
):
    heads = lax.axis_size("head")
    contexts = lax.axis_size("ctx")
    head_number = lax.axis_index("head")
    ctx_number = lax.axis_index("ctx")
    frames = keys.shape[0]
    block = doc_ids.shape[0]
    samples = sample_rows.shape[0]
    per_head = samples // heads
    width = queries.shape[1] // heads
    group = width // HEAD_SIZE
    scale = math.log2(math.e) / math.sqrt(HEAD_SIZE)
    deep = in_proj.shape[1]
    books = targets.shape[1]

    packed = pl.pallas_call(
        functools.partial(pack_kernel, group),
        out_shape=shape_of((heads, 2 * frames + group * per_head, HEAD_SIZE), bf16),
        in_specs=[SMEM, ANY, ANY, ANY],
        out_specs=VMEM,
        scratch_shapes=[
            pltpu.VMEM(queries.shape, bf16),
            pltpu.SemaphoreType.DMA((2 * heads + 4,)),
        ],
        compiler_params=params(56),
        cost_estimate=cost(2 * per_head * frames * queries.shape[1], 2 * 2**20),
    )(sample_rows, keys, values, queries)
    own = to_heads(packed)

    docs, told, mine, info = pl.pallas_call(
        functools.partial(prep_kernel, group),
        out_shape=(
            shape_of((heads, frames), f32),
            shape_of((heads, frames), f32),
            shape_of((samples * group, 128), f32),
            shape_of((8, 128), f32),
        ),
        in_specs=[SMEM, VMEM, VMEM, VMEM],
        out_specs=(VMEM,) * 4,
        compiler_params=params(8),
        cost_estimate=cost(10**6, 4 * 10**5),
    )(
        after(sample_rows, packed),
        doc_ids.reshape(heads, frames),
        owners.reshape(1, samples),
        targets.T,
    )
    ring = [(s, (s + 1) % contexts) for s in range(contexts)]
    half = heads // 2
    before = lax.ppermute(told, "ctx", ring)
    by_head = jnp.transpose(after(queries, packed).reshape(frames, heads, width), (1, 0, 2))
    own, docs, mine, before, by_head = lax.optimization_barrier((own, docs, mine, before, by_head))
    first = own[:half, : 2 * frames].reshape(block, HEAD_SIZE)
    second = own[half:, : 2 * frames].reshape(block, HEAD_SIZE)
    first = lax.ppermute(first, "ctx", ring)
    second = lax.ppermute(second, "ctx", ring)
    queries_here = to_heads(by_head).reshape(block, width)
    pairs = [(s, s + 1 - 2 * (s % 2)) for s in range(heads)]
    other_codes = lax.ppermute(after(code_heads, own), "head", pairs)

    keep, send = pl.pallas_call(
        functools.partial(sample_kernel, scale),
        out_shape=(shape_of((samples // 2, deep), f32), shape_of((samples // 2, deep), bf16)),
        in_specs=[VMEM] * 7,
        out_specs=(VMEM, VMEM),
        scratch_shapes=[pltpu.VMEM((samples * group, 2 * block), f32)],
        compiler_params=params(),
        cost_estimate=cost(
            240 * samples * group * 2 * block * HEAD_SIZE, 4 * 2**20, samples * group * 2 * block
        ),
    )(own, first, second, before, docs, mine, in_proj)
    came = lax.ppermute(send, "head", pairs)

    all_keys, all_values, across, low = pl.pallas_call(
        unpack_kernel,
        out_shape=(
            shape_of((2 * block, HEAD_SIZE), bf16),
            shape_of((2 * block, HEAD_SIZE), bf16),
            shape_of((2 * heads, frames), f32),
            shape_of((block // HEAD_SIZE,), jnp.int32),
        ),
        in_specs=[VMEM] * 5,
        out_specs=(VMEM, VMEM, VMEM, SMEM),
        compiler_params=params(),
        cost_estimate=cost(0, 2 * 2**20),
    )(after(own, send), first, second, before, docs)

    came, all_keys, all_values = lax.optimization_barrier((came, all_keys, all_values))
    shares = pl.pallas_call(
        pair_kernel,
        out_shape=shape_of((heads // 2, samples // 2, deep), bf16),
        in_specs=[VMEM] * 2,
        out_specs=VMEM,
        compiler_params=params(),
        cost_estimate=cost(samples * deep, 4 * samples * deep),
    )(keep, came)
    parts = lax.all_to_all(
        after(shares, queries_here),
        "head",
        split_axis=0,
        concat_axis=0,
        tiled=True,
        axis_index_groups=[list(range(core, heads, 2)) for core in range(2)],
    )
    tiles = block // HEAD_SIZE
    run = functools.partial(attend, scale)
    first_end = CUT
    attended = run(0, first_end, low, queries_here, all_keys, all_values, across, None)
    parts, attended = lax.optimization_barrier((parts, attended))
    codes_here = code_heads.shape[2]
    stats = pl.pallas_call(
        logits_kernel,
        out_shape=shape_of((heads, 8, 128), f32),
        in_specs=[VMEM] * 5,
        out_specs=VMEM,
        compiler_params=params(),
        cost_estimate=cost(4 * samples * deep * codes_here * books, code_heads.size * 4),
    )(parts, dec_gain[None, :], code_heads, other_codes, info)
    attended = run(
        first_end,
        tiles - first_end,
        after(low, stats),
        queries_here,
        all_keys,
        all_values,
        across,
        attended,
    )
    all_stats = to_heads(stats)

    all_stats, attended = lax.optimization_barrier((all_stats, attended))
    slot_count = 2 * contexts
    placed = pl.pallas_call(
        functools.partial(place_kernel, books, samples),
        out_shape=shape_of((contexts, slot_count), f32),
        in_specs=[VMEM] * 2,
        out_specs=VMEM,
        compiler_params=params(8),
        cost_estimate=cost(10**6, 10**5),
    )(all_stats, info)
    arrived = lax.all_to_all(placed, "ctx", split_axis=0, concat_axis=0, tiled=True)
    slot_loss = jnp.sum(arrived, axis=0, keepdims=True)
    return (attended, slot_loss)


def solution(mesh):
    in_specs = (
        P(("ctx", "head"), None),
        P(("ctx", "head"), None),
        P(("ctx", "head"), None),
        P("ctx"),
        P("ctx"),
        P("ctx", None),
        P("ctx", None),
        P("head", None),
        P(),
        P(None, None, "head"),
    )
    out_specs = (P("ctx", "head"), P("ctx", None))
    return jax.shard_map(local, mesh=mesh, in_specs=in_specs, out_specs=out_specs, check_vma=False)
```

time: 109 us -> 102 us (0.936)
  waiting for transfers between devices: 31.7 us -> 17.3 us
  starting transfers between devices: 28 us -> 34.7 us
  other arithmetic: 1.87 us -> 0.59 us
    all_to_all x4 -> x3, waiting for transfers between devices: 18.7 us -> 0.01 us  [to_heads(): lax.all_to_all(value, 'head', split_axis=0, concat_axis=0, tiled=True)]
    ppermute x0 -> x3, starting transfers between devices: none -> 7.2 us  [the longest x1 3.36 us: local(): came = lax.ppermute(send, 'head', pairs)]
    ppermute x0 -> x3, waiting for transfers between devices: none -> 6.96 us  [the longest x1 6.95 us: local(): before = lax.ppermute(told, 'ctx', ring)]
    ppermute x1, waiting for transfers between devices: 7.3 us -> 2.22 us  [local(): first = lax.ppermute(first, 'ctx', ring)]
    all_to_all x4 -> x3, starting transfers between devices: 24.2 us -> 20.2 us  [to_heads(): lax.all_to_all(value, 'head', split_axis=0, concat_axis=0, tiled=True)]
    all_to_all x0 -> x1, starting transfers between devices: none -> 3.41 us  [local(): lax.all_to_all(after(shares, queries_here), 'head', split_axis=0, concat_...]
    all_to_all x0 -> x1, waiting for transfers between devices: none -> 2.5 us  [local(): lax.all_to_all(after(shares, queries_here), 'head', split_axis=0, concat_...]
    unnamed x25 -> x26, local copies, waits for them, and re-layouts: 4.06 us -> 5.6 us
  transfers between devices with their start and end apart: 6 -> 9, of which waited for: 5 -> 4; matrix products, arithmetic and copies ran while one was open for 5% -> 1% of each run, Pallas kernels for 10% -> 12%
where the time goes in v2:
time: 102 us; the launch traced here: 101 us
  starting transfers between devices  34.7 us (34%)
  blocking collectives  23.2 us (23%)
  waiting for transfers between devices  17.3 us (17%)
  Pallas kernels  16.6 us (16%)
  local copies, waits for them, and re-layouts  7.52 us (7%)
    all_to_all x1, blocking collectives, local(): lax.all_to_all(placed, 'ctx', split_axis=0, concat_axis=0, tiled=True)  23.2 us
    all_to_all x3, starting transfers between devices, to_heads(): lax.all_to_all(value, 'head', split_axis=0, concat_axis=0, tiled=True)  20.2 us
    pallas_call x2, Pallas kernels, attend(): pl.pallas_call(functools.partial(main_kernel, scale, first_tile), grid=(t...  7.29 us
    ppermute x1, waiting for transfers between devices, local(): before = lax.ppermute(told, 'ctx', ring)  6.95 us
    ppermute x1, waiting for transfers between devices, local(): second = lax.ppermute(second, 'ctx', ring)  5.62 us
    unnamed x26, local copies, waits for them, and re-layouts  5.6 us
    all_to_all x1, starting transfers between devices, local(): lax.all_to_all(after(shares, queries_here), 'head', split_axis=0, concat_...  3.41 us
    ppermute x1, starting transfers between devices, local(): came = lax.ppermute(send, 'head', pairs)  3.36 us
  transfers between devices with their start and end apart: 9, of which 4 were waited for; matrix products, arithmetic and copies ran while one was open for 1% of the time, Pallas kernels for 12%

profile of v2, /device:TPU:1, one launch (start us, length us, event | category | flops | bytes accessed | tf_op | source)
XLA Modules:
  0.0 100.8 jit_solution(25885358981166758)
XLA Ops:
  0.6 3.2 %shard_map.113 = bf16[8,288,128]{2,1,0:T(8,128)(2,1)} custom-call(s32[64]{0:T(128)} %rows_ref.2, bf16[128,1024]{1,0:T(8,128)(2,1)} %keys_hbm.1, bf16[128,1024]{1,0:T(8,128)(2,1)} %values_hbm.1, bf16[128,4096]{1,0:T(8,128)(2,1)} %queries_hbm.1), custom_call_target="tpu_custom_call" | custom-call | flops 8388608 | bytes 2097152 | tf_op jit(solution)/shard_map/pallas_call | solution.py:399
  3.8 10.5 %all-to-all-start = ((bf16[8,288,128]{2,1,0:T(8,128)(2,1)}), bf16[8,288,128]{2,1,0:T(8,128)(2,1)S(1)}, u32[]{:S(2)}, u32[]{:S(2)}) async-start(bf16[8,288,128]{2,1,0:T(8,128)(2,1)} %shard_map.113), calls=%async_computation | async-start | bytes 1179648 | tf_op jit(solution)/shard_map/all_to_all | solution.py:375
  14.3 0.7 copy-done.2
  15.0 0.7 shard_map.114
  15.6 1.9 %collective-permute-start = (f32[8,128]{1,0:T(8,128)S(1)}, f32[8,128]{1,0:T(8,128)S(1)}, u32[]{:S(2)}, u32[]{:S(2)}) collective-permute-start(f32[8,128]{1,0:T(8,128)S(1)} %get-tuple-element.33), channel_id=1, source_target_pairs={{0,8},{8,16},{16,24},{24,32},{32,40},{40,48},{48,56},{56,64},{64,7... | collective-permute-start | bytes 12296 | tf_op jit(solution)/shard_map/ppermute | solution.py:433
  17.6 1.1 %copy.18 = bf16[16,8,8,512]{3,2,0,1:T(8,128)(2,1)} copy(bf16[16,8,8,512]{3,2,1,0:T(8,128)(2,1)S(1)} %bitcast.23) | data formatting | bytes 2097152 | tf_op jit(solution)/shard_map/reshape | solution.py:434
  18.7 7.0 %collective-permute-done.before_ref = f32[8,128]{1,0:T(8,128)S(1)} collective-permute-done((f32[8,128]{1,0:T(8,128)S(1)}, f32[8,128]{1,0:T(8,128)S(1)}, u32[]{:S(2)}, u32[]{:S(2)}) %collective-permute-start) | collective-permute-done | bytes 4128 | tf_op jit(solution)/shard_map/ppermute | solution.py:433
  25.6 0.8 fusion
  26.5 1.9 %collective-permute-start.1 = (bf16[1024,128]{1,0:T(8,128)(2,1)}, bf16[1024,128]{1,0:T(8,128)(2,1)S(1)}, u32[]{:S(2)}, u32[]{:S(2)}) collective-permute-start(bf16[1024,128]{1,0:T(8,128)(2,1)} %bitcast.4), channel_id=1, source_target_pairs={{0,8},{8,16},{16,24},{24,32},{32,40},{40,48},{48,56},{56,64},{64,7... | collective-permute-start | bytes 786440 | tf_op jit(solution)/shard_map/ppermute | solution.py:438
  28.4 2.1 %collective-permute-start.2 = (bf16[1024,128]{1,0:T(8,128)(2,1)}, bf16[1024,128]{1,0:T(8,128)(2,1)S(1)}, u32[]{:S(2)}, u32[]{:S(2)}) collective-permute-start(bf16[1024,128]{1,0:T(8,128)(2,1)} %bitcast.5), channel_id=1, source_target_pairs={{0,8},{8,16},{16,24},{24,32},{32,40},{40,48},{48,56},{56,64},{64,7... | collective-permute-start | bytes 786440 | tf_op jit(solution)/shard_map/ppermute | solution.py:439
  30.4 5.7 %all-to-all-start.1 = ((bf16[8,128,512]{2,1,0:T(8,128)(2,1)}), bf16[8,128,512]{2,1,0:T(8,128)(2,1)}, u32[]{:S(2)}, u32[]{:S(2)}) async-start(bf16[8,128,512]{2,1,0:T(8,128)(2,1)} %bitcast.17), calls=%async_computation.1 | async-start | bytes 2097152 | tf_op jit(solution)/shard_map/all_to_all | solution.py:375
  36.1 1.9 %collective-permute-start.4 = (bf16[2,1024,256]{2,1,0:T(8,128)(2,1)S(1)}, bf16[2,1024,256]{2,1,0:T(8,128)(2,1)S(1)}, u32[]{:S(2)}, u32[]{:S(2)}) collective-permute-start(bf16[2,1024,256]{2,1,0:T(8,128)(2,1)S(1)} %copy-done), channel_id=1, source_target_pairs={{0,1},{1,0},{2,3},{3,2},{4,5},{5,4},{6,7},{7,6},{8,9},{9,8},{10,11... | collective-permute-start | bytes 3145736 | tf_op jit(solution)/shard_map/ppermute | solution.py:442
  38.1 2.2 %collective-permute-done.1.first_ref = bf16[1024,128]{1,0:T(8,128)(2,1)S(1)} collective-permute-done((bf16[1024,128]{1,0:T(8,128)(2,1)}, bf16[1024,128]{1,0:T(8,128)(2,1)S(1)}, u32[]{:S(2)}, u32[]{:S(2)}) %collective-permute-start.1) | collective-permute-done | bytes 262176 | tf_op jit(solution)/shard_map/ppermute | solution.py:438
  40.3 5.6 %collective-permute-done.2.second_ref = bf16[1024,128]{1,0:T(8,128)(2,1)S(1)} collective-permute-done((bf16[1024,128]{1,0:T(8,128)(2,1)}, bf16[1024,128]{1,0:T(8,128)(2,1)S(1)}, u32[]{:S(2)}, u32[]{:S(2)}) %collective-permute-start.2) | collective-permute-done | bytes 262176 | tf_op jit(solution)/shard_map/ppermute | solution.py:439
  45.9 1.2 %copy-done.6 = bf16[512,1024]{1,0:T(8,128)(2,1)S(1)} copy-done((bf16[512,1024]{1,0:T(8,128)(2,1)S(1)}, bf16[512,1024]{1,0:T(8,128)(2,1)}, u32[]{:S(2)}) %copy-start.6) | copy-done | bytes 1048600
  47.1 1.6 %shard_map.115 = (f32[32,1024]{1,0:T(8,128)S(1)}, bf16[32,1024]{1,0:T(8,128)(2,1)S(1)}) custom-call(bf16[8,288,128]{2,1,0:T(8,128)(2,1)S(1)} %all-to-all-done.own_ref, bf16[1024,128]{1,0:T(8,128)(2,1)S(1)} %collective-permute-done.1.first_ref, bf16[1024,128]{1,0:T(8,128)(2,1)S(1)} %collective-permute-done.2.second_ref, ...), custom_call_target="tpu_custom_call" | custom-call | flops 16106127360 | bytes 4194304 | tf_op jit(solution)/shard_map/pallas_call | solution.py:444
  48.7 3.4 %collective-permute-start.3 = (bf16[32,1024]{1,0:T(8,128)(2,1)S(1)}, bf16[32,1024]{1,0:T(8,128)(2,1)S(1)}, u32[]{:S(2)}, u32[]{:S(2)}) collective-permute-start(bf16[32,1024]{1,0:T(8,128)(2,1)S(1)} %get-tuple-element.40), channel_id=1, source_target_pairs={{0,1},{1,0},{2,3},{3,2},{4,5},{5,4},{6,7},{7,6},{8,9},{9,8},{10,11... | collective-permute-start | bytes 196616 | tf_op jit(solution)/shard_map/ppermute | solution.py:455
  52.0 1.6 %shard_map.116 = (bf16[2048,128]{1,0:T(8,128)(2,1)S(1)}, bf16[2048,128]{1,0:T(8,128)(2,1)S(1)}, f32[16,128]{1,0:T(8,128)S(1)}, s32[8]{0:T(128)S(1)}) custom-call(bf16[8,288,128]{2,1,0:T(8,128)(2,1)S(1)} %all-to-all-done.own_ref, bf16[1024,128]{1,0:T(8,128)(2,1)S(1)} %collective-permute-done.1.first_ref, ...), custom_call_target="tpu_custom_call" | custom-call | bytes 2097152 | tf_op jit(solution)/shard_map/pallas_call | solution.py:457
  53.7 0.8 copy-done.7
  54.5 0.8 copy-done.9
  55.3 0.7 shard_map.117
  56.0 3.4 %all-to-all-start.2 = ((bf16[4,32,1024]{2,1,0:T(8,128)(2,1)}), bf16[4,32,1024]{2,1,0:T(8,128)(2,1)S(1)}, u32[]{:S(2)}, u32[]{:S(2)}) async-start(bf16[4,32,1024]{2,1,0:T(8,128)(2,1)} %shard_map.117), calls=%async_computation.2 | async-start | bytes 524288 | tf_op jit(solution)/shard_map/all_to_all | solution.py:480
  59.5 1.0 %copy-done.10 = bf16[2048,128]{1,0:T(8,128)(2,1)S(1)} copy-done((bf16[2048,128]{1,0:T(8,128)(2,1)S(1)}, bf16[2048,128]{1,0:T(8,128)(2,1)}, u32[]{:S(2)}) %copy-start.10) | copy-done | bytes 524312
  60.5 3.2 %shard_map.118.refs_0_ = bf16[1024,512]{1,0:T(8,128)(2,1)} custom-call(s32[8]{0:T(128)S(1)} %get-tuple-element.54.low_ref, bf16[1024,512]{1,0:T(8,128)(2,1)} %bitcast.6.queries_ref, bf16[2048,128]{1,0:T(8,128)(2,1)S(1)} %copy-done.8, bf16[2048,128]{1,0:T(8,128)(2,1)S(1)} %copy-done.10, f32[16,128]{1,0:T(8,128)S(1)} %get-tuple-element.50.across_ref), custom_call_target="tpu_custom_call" | custom-call | flops 1610612736 | bytes 2097152 | tf_op jit(solution)/shard_map/pallas_call | solution.py:358
  63.7 2.5 %all-to-all-done.2.parts_ref = bf16[4,32,1024]{2,1,0:T(8,128)(2,1)S(1)} async-done(((bf16[4,32,1024]{2,1,0:T(8,128)(2,1)}), bf16[4,32,1024]{2,1,0:T(8,128)(2,1)S(1)}, u32[]{:S(2)}, u32[]{:S(2)}) %all-to-all-start.2) | async-done | bytes 262176 | tf_op jit(solution)/shard_map/all_to_all | solution.py:480
  66.2 1.4 %shard_map.119 = f32[8,8,128]{2,1,0:T(8,128)} custom-call(bf16[4,32,1024]{2,1,0:T(8,128)(2,1)S(1)} %all-to-all-done.2.parts_ref, f32[1,1024]{1,0:T(1,128)S(1)} %bitcast.19, bf16[2,1024,256]{2,1,0:T(8,128)(2,1)S(1)} %copy-done, bf16[2,1024,256]{2,1,0:T(8,128)(2,1)S(1)} %collective-permute-done.4.other_ref, f32[8,128]{1,0:T(8,128)S(1)} %get-tuple-element.53.info_ref), custom_call_target="tpu_custom_call" | custom-call | flops 134217728 | bytes 2097152 | tf_op jit(solution)/shard_map/pallas_call | solution.py:494
  67.6 4.0 %all-to-all-start.3 = ((f32[8,8,128]{2,1,0:T(8,128)}), f32[8,8,128]{2,1,0:T(8,128)S(1)}, u32[]{:S(2)}, u32[]{:S(2)}) async-start(f32[8,8,128]{2,1,0:T(8,128)} %shard_map.119), calls=%async_computation.3 | async-start | bytes 65536 | tf_op jit(solution)/shard_map/all_to_all | solution.py:375
  71.6 1.0 %copy-done.11 = bf16[2048,128]{1,0:T(8,128)(2,1)S(1)} copy-done((bf16[2048,128]{1,0:T(8,128)(2,1)S(1)}, bf16[2048,128]{1,0:T(8,128)(2,1)}, u32[]{:S(2)}) %copy-start.11) | copy-done | bytes 524312
  72.7 4.0 %shard_map.120 = bf16[1024,512]{1,0:T(8,128)(2,1)} custom-call(s32[8]{0:T(128)S(1)} %get-tuple-element.54.low_ref, bf16[1024,512]{1,0:T(8,128)(2,1)} %bitcast.6.queries_ref, bf16[2048,128]{1,0:T(8,128)(2,1)S(1)} %copy-done.8, bf16[2048,128]{1,0:T(8,128)(2,1)S(1)} %copy-done.11, ...), custom_call_target="tpu_custom_call", output_to_operand_aliasing={{}: (5, {})} | custom-call | flops 1610612736 | bytes 2097152 | tf_op jit(solution)/shard_map/pallas_call | solution.py:358
  76.7 0.3 shard_map.121
  77.0 23.2 %all_to_all.29 = f32[64,1,128]{2,1,0:T(1,128)S(1)} all-to-all(f32[64,1,128]{2,1,0:T(1,128)S(1)} %bitcast.18), channel_id=1, replica_groups=mesh['ctx'=64,'head'=8] {'ctx'}, dimensions={0} | all-to-all | bytes 65536 | tf_op jit(solution)/shard_map/all_to_all | solution.py:524
  100.2 0.6 reduce_sum.9
  (25 shorter events, 0.1 us)
Async XLA Ops:
  3.8 10.5 %copy-start.5 = (s32[64,1]{0,1:T(1,128)S(1)}, s32[64,1]{0,1:T(1,128)}, u32[]{:S(2)}) copy-start(s32[64,1]{0,1:T(1,128)} %param.15) | copy-start | bytes 772
  3.8 13.8 %copy-start.12 = (bf16[128,4096]{1,0:T(8,128)(2,1)S(1)}, bf16[128,4096]{1,0:T(8,128)(2,1)}, u32[]{:S(2)}) copy-start(bf16[128,4096]{1,0:T(8,128)(2,1)} %queries_hbm.1) | copy-start | bytes 3145732
  3.8 21.8 %all-to-all-start = ((bf16[8,288,128]{2,1,0:T(8,128)(2,1)}), bf16[8,288,128]{2,1,0:T(8,128)(2,1)S(1)}, u32[]{:S(2)}, u32[]{:S(2)}) async-start(bf16[8,288,128]{2,1,0:T(8,128)(2,1)} %shard_map.113), calls=%async_computation | async-start | bytes 1179648 | tf_op jit(solution)/shard_map/all_to_all | solution.py:375
  14.3 0.7 copy-start.2
  14.3 0.7 copy-start.3
  14.3 0.7 copy-start.4
  15.6 10.0 %collective-permute-start = (f32[8,128]{1,0:T(8,128)S(1)}, f32[8,128]{1,0:T(8,128)S(1)}, u32[]{:S(2)}, u32[]{:S(2)}) collective-permute-start(f32[8,128]{1,0:T(8,128)S(1)} %get-tuple-element.33), channel_id=1, source_target_pairs={{0,8},{8,16},{16,24},{24,32},{32,40},{40,48},{48,56},{56,64},{64,7... | collective-permute-start | bytes 12296 | tf_op jit(solution)/shard_map/ppermute | solution.py:433
  26.5 13.8 %collective-permute-start.1 = (bf16[1024,128]{1,0:T(8,128)(2,1)}, bf16[1024,128]{1,0:T(8,128)(2,1)S(1)}, u32[]{:S(2)}, u32[]{:S(2)}) collective-permute-start(bf16[1024,128]{1,0:T(8,128)(2,1)} %bitcast.4), channel_id=1, source_target_pairs={{0,8},{8,16},{16,24},{24,32},{32,40},{40,48},{48,56},{56,64},{64,7... | collective-permute-start | bytes 786440 | tf_op jit(solution)/shard_map/ppermute | solution.py:438
  28.4 7.8 %copy-start = (bf16[2,1024,256]{2,1,0:T(8,128)(2,1)S(1)}, bf16[2,1024,256]{2,1,0:T(8,128)(2,1)}, u32[]{:S(2)}) copy-start(bf16[2,1024,256]{2,1,0:T(8,128)(2,1)} %codes_ref.1) | copy-start | bytes 3145732
  28.4 17.5 %collective-permute-start.2 = (bf16[1024,128]{1,0:T(8,128)(2,1)}, bf16[1024,128]{1,0:T(8,128)(2,1)S(1)}, u32[]{:S(2)}, u32[]{:S(2)}) collective-permute-start(bf16[1024,128]{1,0:T(8,128)(2,1)} %bitcast.5), channel_id=1, source_target_pairs={{0,8},{8,16},{16,24},{24,32},{32,40},{40,48},{48,56},{56,64},{64,7... | collective-permute-start | bytes 786440 | tf_op jit(solution)/shard_map/ppermute | solution.py:439
  30.4 25.6 %all-to-all-start.1 = ((bf16[8,128,512]{2,1,0:T(8,128)(2,1)}), bf16[8,128,512]{2,1,0:T(8,128)(2,1)}, u32[]{:S(2)}, u32[]{:S(2)}) async-start(bf16[8,128,512]{2,1,0:T(8,128)(2,1)} %bitcast.17), calls=%async_computation.1 | async-start | bytes 2097152 | tf_op jit(solution)/shard_map/all_to_all | solution.py:375
  36.1 30.1 %collective-permute-start.4 = (bf16[2,1024,256]{2,1,0:T(8,128)(2,1)S(1)}, bf16[2,1024,256]{2,1,0:T(8,128)(2,1)S(1)}, u32[]{:S(2)}, u32[]{:S(2)}) collective-permute-start(bf16[2,1024,256]{2,1,0:T(8,128)(2,1)S(1)} %copy-done), channel_id=1, source_target_pairs={{0,1},{1,0},{2,3},{3,2},{4,5},{5,4},{6,7},{7,6},{8,9},{9,8},{10,11... | collective-permute-start | bytes 3145736 | tf_op jit(solution)/shard_map/ppermute | solution.py:442
  45.9 1.2 %copy-start.6 = (bf16[512,1024]{1,0:T(8,128)(2,1)S(1)}, bf16[512,1024]{1,0:T(8,128)(2,1)}, u32[]{:S(2)}) copy-start(bf16[512,1024]{1,0:T(8,128)(2,1)} %proj_ref.1) | copy-start | bytes 3145732
  48.7 6.6 %collective-permute-start.3 = (bf16[32,1024]{1,0:T(8,128)(2,1)S(1)}, bf16[32,1024]{1,0:T(8,128)(2,1)S(1)}, u32[]{:S(2)}, u32[]{:S(2)}) collective-permute-start(bf16[32,1024]{1,0:T(8,128)(2,1)S(1)} %get-tuple-element.40), channel_id=1, source_target_pairs={{0,1},{1,0},{2,3},{3,2},{4,5},{5,4},{6,7},{7,6},{8,9},{9,8},{10,11... | collective-permute-start | bytes 196616 | tf_op jit(solution)/shard_map/ppermute | solution.py:455
  53.7 0.8 copy-start.7
  54.5 0.8 copy-start.9
  55.3 4.1 %copy-start.8 = (bf16[2048,128]{1,0:T(8,128)(2,1)S(1)}, bf16[2048,128]{1,0:T(8,128)(2,1)}, u32[]{:S(2)}) copy-start(bf16[2048,128]{1,0:T(8,128)(2,1)} %copy-done.7) | copy-start | bytes 1572868
  56.0 10.2 %all-to-all-start.2 = ((bf16[4,32,1024]{2,1,0:T(8,128)(2,1)}), bf16[4,32,1024]{2,1,0:T(8,128)(2,1)S(1)}, u32[]{:S(2)}, u32[]{:S(2)}) async-start(bf16[4,32,1024]{2,1,0:T(8,128)(2,1)} %shard_map.117), calls=%async_computation.2 | async-start | bytes 524288 | tf_op jit(solution)/shard_map/all_to_all | solution.py:480
  59.4 1.0 %copy-start.10 = (bf16[2048,128]{1,0:T(8,128)(2,1)S(1)}, bf16[2048,128]{1,0:T(8,128)(2,1)}, u32[]{:S(2)}) copy-start(bf16[2048,128]{1,0:T(8,128)(2,1)} %copy-done.9) | copy-start | bytes 1572868
  60.5 5.7 %copy-start.1 = (f32[1024]{0:T(1024)S(1)}, f32[1024]{0:T(1024)}, u32[]{:S(2)}) copy-start(f32[1024]{0:T(1024)} %param.18) | copy-start | bytes 12292
  67.6 9.1 %all-to-all-start.3 = ((f32[8,8,128]{2,1,0:T(8,128)}), f32[8,8,128]{2,1,0:T(8,128)S(1)}, u32[]{:S(2)}, u32[]{:S(2)}) async-start(f32[8,8,128]{2,1,0:T(8,128)} %shard_map.119), calls=%async_computation.3 | async-start | bytes 65536 | tf_op jit(solution)/shard_map/all_to_all | solution.py:375
  71.6 1.0 %copy-start.11 = (bf16[2048,128]{1,0:T(8,128)(2,1)S(1)}, bf16[2048,128]{1,0:T(8,128)(2,1)}, u32[]{:S(2)}) copy-start(bf16[2048,128]{1,0:T(8,128)(2,1)} %copy-done.9) | copy-start | bytes 1572868

commit v3 on v2

--- a/solution.py
+++ b/solution.py
@@ -114,36 +114,26 @@
     info_ref[1:2, :] = rank + (2 * lax.axis_index("ctx")).astype(f32)
 
 
-def block_rows(s, own_ref, first_ref, second_ref, frames, which):
+def block_rows(s, own_ref, halo_ref, frames, which):
     heads = own_ref.shape[0]
-    half = heads // 2
     if s >= heads:
         return own_ref[s - heads, pl.ds(which * frames, frames), :]
-    ref, at = (first_ref, s) if s < half else (second_ref, s - half)
-    return ref[pl.ds((2 * at + which) * frames, frames), :]
-
-
-def unpack_kernel(
-    own_ref, first_ref, second_ref, before_ref, docs_ref, keys_ref, values_ref, all_docs_ref, low_ref
-):
-    heads = own_ref.shape[0]
-    frames = docs_ref.shape[1]
-    for s in range(2 * heads):
-        rows = pl.ds(s * frames, frames)
-        keys_ref[rows, :] = block_rows(s, own_ref, first_ref, second_ref, frames, 0)
-        values_ref[rows, :] = block_rows(s, own_ref, first_ref, second_ref, frames, 1)
+    return halo_ref[pl.ds((2 * s + which) * frames, frames), :]
+
+
+def window_kernel(before_ref, docs_ref, all_docs_ref, low_ref):
     docs = jnp.concatenate([before_ref[...], docs_ref[...]], axis=0)
     all_docs_ref[...] = docs
     for t in range(low_ref.shape[0]):
-        below = jnp.where(docs < docs_ref[t : t + 1, 0:1], 1.0, 0.0)
+        first = docs_ref[t * QUERY_TILE // HEAD_SIZE : t * QUERY_TILE // HEAD_SIZE + 1, 0:1]
+        below = jnp.where(docs < first, 1.0, 0.0)
         low_ref[t] = jnp.sum(below).astype(jnp.int32) // KEY_TILE
 
 
 def sample_kernel(
     scale,
     own_ref,
-    first_ref,
-    second_ref,
+    halo_ref,
     before_ref,
     docs_ref,
     mine_ref,
@@ -167,7 +157,7 @@
     highest = jnp.full((rows, HEAD_SIZE), MASKED, f32)
     for s in range(0, 2 * heads, 2):
         key_tile = jnp.concatenate(
-            [block_rows(s + i, own_ref, first_ref, second_ref, frames, 0) for i in range(2)], axis=0
+            [block_rows(s + i, own_ref, halo_ref, frames, 0) for i in range(2)], axis=0
         )
         scores = lax.dot_general(
             queries, key_tile, (((1,), (1,)), ((), ())), preferred_element_type=f32
@@ -184,7 +174,7 @@
     mixed = jnp.zeros((rows, HEAD_SIZE), f32)
     for s in range(0, 2 * heads, 2):
         value_tile = jnp.concatenate(
-            [block_rows(s + i, own_ref, first_ref, second_ref, frames, 1) for i in range(2)], axis=0
+            [block_rows(s + i, own_ref, halo_ref, frames, 1) for i in range(2)], axis=0
         )
         start = s * frames
         weights = jnp.exp2(scores_ref[:, start : start + tile] - top)
@@ -273,18 +263,30 @@
     )
 
 
-def main_kernel(scale, first_tile, low_ref, queries_ref, keys_ref, values_ref, across_ref, *refs):
-    out_ref, bias_ref, scores_ref = refs[-3:]
+def main_kernel(scale, first_tile, steps, low_ref, queries_ref, own_ref, halo_ref, across_ref, *refs):
+    out_ref, bias_ref, scores_ref, keys_ref, values_ref = refs[-5:]
     tile, width = queries_ref.shape
     group = width // HEAD_SIZE
     parts = tile // HEAD_SIZE
     block = keys_ref.shape[0] // 2
     number = first_tile + pl.program_id(0)
     start = block + number * tile
-    low = low_ref[number * parts]
+    low = low_ref[number]
     high = (start + tile + KEY_TILE - 1) // KEY_TILE
     halves = KEY_TILE // HEAD_SIZE
     units = [(j, r) for j in range(group) for r in range(parts)]
+    frames = HEAD_SIZE
+    sources = 2 * block // frames
+    first_source = first_tile * parts
+    last_source = sources // 2 + (first_tile + steps) * parts
+
+    @pl.when(pl.program_id(0) == 0)
+    def _():
+        for s in range(first_source, last_source):
+            rows = pl.ds(s * frames, frames)
+            keys_ref[rows, :] = block_rows(s, own_ref, halo_ref, frames, 0)
+            values_ref[rows, :] = block_rows(s, own_ref, halo_ref, frames, 1)
+
 
     def body(count):
         base = pl.multiple_of(low * KEY_TILE, KEY_TILE)
@@ -333,7 +335,7 @@
         pl.when(high - low == count)(functools.partial(body, count))
 
 
-def attend(scale, first_tile, tiles, low, queries, keys, values, across, before):
+def attend(scale, first_tile, tiles, low, queries, own, halo, across, before):
     block, width = queries.shape
     tile = QUERY_TILE
     first_tile, tiles = first_tile * HEAD_SIZE // tile, tiles * HEAD_SIZE // tile
@@ -344,11 +346,11 @@
     in_specs = [
         SMEM,
         pl.BlockSpec((tile, width), rows),
-        pl.BlockSpec(keys.shape, whole),
-        pl.BlockSpec(values.shape, whole),
+        pl.BlockSpec(own.shape, lambda i: (0, 0, 0)),
+        pl.BlockSpec(halo.shape, whole),
         pl.BlockSpec(across.shape, whole),
     ]
-    operands = [low, queries, keys, values, across]
+    operands = [low, queries, own, halo, across]
     aliases = {}
     if before is not None:
         in_specs.append(pl.BlockSpec(memory_space=pl.ANY))
@@ -356,7 +358,7 @@
         aliases = {len(operands) - 1: 0}
     pairs = tiles * group * tile * 4 * KEY_TILE
     return pl.pallas_call(
-        functools.partial(main_kernel, scale, first_tile),
+        functools.partial(main_kernel, scale, first_tile, tiles),
         grid=(tiles,),
         out_shape=shape_of((block, width), bf16),
         in_specs=in_specs,
@@ -364,6 +366,8 @@
         scratch_shapes=[
             pltpu.VMEM((tile // HEAD_SIZE, HEAD_SIZE, most * KEY_TILE), f32),
             pltpu.VMEM((group * tile // HEAD_SIZE, HEAD_SIZE, most * KEY_TILE), f32),
+            pltpu.VMEM((2 * block, HEAD_SIZE), bf16),
+            pltpu.VMEM((2 * block, HEAD_SIZE), bf16),
         ],
         input_output_aliases=aliases,
         compiler_params=params(),
@@ -429,46 +433,39 @@
         targets.T,
     )
     ring = [(s, (s + 1) % contexts) for s in range(contexts)]
-    half = heads // 2
     before = lax.ppermute(told, "ctx", ring)
     by_head = jnp.transpose(after(queries, packed).reshape(frames, heads, width), (1, 0, 2))
     own, docs, mine, before, by_head = lax.optimization_barrier((own, docs, mine, before, by_head))
-    first = own[:half, : 2 * frames].reshape(block, HEAD_SIZE)
-    second = own[half:, : 2 * frames].reshape(block, HEAD_SIZE)
-    first = lax.ppermute(first, "ctx", ring)
-    second = lax.ppermute(second, "ctx", ring)
+    halo = lax.ppermute(own[:, : 2 * frames].reshape(2 * block, HEAD_SIZE), "ctx", ring)
     queries_here = to_heads(by_head).reshape(block, width)
     pairs = [(s, s + 1 - 2 * (s % 2)) for s in range(heads)]
     other_codes = lax.ppermute(after(code_heads, own), "head", pairs)
 
+    across, low = pl.pallas_call(
+        window_kernel,
+        out_shape=(
+            shape_of((2 * heads, frames), f32),
+            shape_of((block // QUERY_TILE,), jnp.int32),
+        ),
+        in_specs=[VMEM] * 2,
+        out_specs=(VMEM, SMEM),
+        compiler_params=params(8),
+        cost_estimate=cost(0, 2 * 2**16),
+    )(before, docs)
+    halo, across, low = lax.optimization_barrier((halo, across, low))
     keep, send = pl.pallas_call(
         functools.partial(sample_kernel, scale),
         out_shape=(shape_of((samples // 2, deep), f32), shape_of((samples // 2, deep), bf16)),
-        in_specs=[VMEM] * 7,
+        in_specs=[VMEM] * 6,
         out_specs=(VMEM, VMEM),
         scratch_shapes=[pltpu.VMEM((samples * group, 2 * block), f32)],
         compiler_params=params(),
         cost_estimate=cost(
             240 * samples * group * 2 * block * HEAD_SIZE, 4 * 2**20, samples * group * 2 * block
         ),
-    )(own, first, second, before, docs, mine, in_proj)
+    )(own, halo, before, docs, mine, in_proj)
     came = lax.ppermute(send, "head", pairs)
 
-    all_keys, all_values, across, low = pl.pallas_call(
-        unpack_kernel,
-        out_shape=(
-            shape_of((2 * block, HEAD_SIZE), bf16),
-            shape_of((2 * block, HEAD_SIZE), bf16),
-            shape_of((2 * heads, frames), f32),
-            shape_of((block // HEAD_SIZE,), jnp.int32),
-        ),
-        in_specs=[VMEM] * 5,
-        out_specs=(VMEM, VMEM, VMEM, SMEM),
-        compiler_params=params(),
-        cost_estimate=cost(0, 2 * 2**20),
-    )(after(own, send), first, second, before, docs)
-
-    came, all_keys, all_values = lax.optimization_barrier((came, all_keys, all_values))
     shares = pl.pallas_call(
         pair_kernel,
         out_shape=shape_of((heads // 2, samples // 2, deep), bf16),
@@ -488,7 +485,7 @@
     tiles = block // HEAD_SIZE
     run = functools.partial(attend, scale)
     first_end = CUT
-    attended = run(0, first_end, low, queries_here, all_keys, all_values, across, None)
+    attended = run(0, first_end, low, queries_here, own, halo, across, None)
     parts, attended = lax.optimization_barrier((parts, attended))
     codes_here = code_heads.shape[2]
     stats = pl.pallas_call(
@@ -504,8 +501,8 @@
         tiles - first_end,
         after(low, stats),
         queries_here,
-        all_keys,
-        all_values,
+        own,
+        halo,
         across,
         attended,
     )

time: 102 us -> 98.3 us (0.964)
  local copies, waits for them, and re-layouts: 7.52 us -> 3.86 us
  waiting for transfers between devices: 17.3 us -> 20.2 us
  starting transfers between devices: 34.7 us -> 33.5 us
    unnamed x26 -> x16, local copies, waits for them, and re-layouts: 5.6 us -> 1.94 us
    ppermute x2 -> x1, starting transfers between devices: 3.96 us -> 2.04 us  [local(): lax.ppermute(own[:, :2 * frames].reshape(2 * block, HEAD_SIZE), 'ctx', ring)]
    ppermute x2 -> x1, waiting for transfers between devices: 7.84 us -> 8.79 us  [local(): lax.ppermute(own[:, :2 * frames].reshape(2 * block, HEAD_SIZE), 'ctx', ring)]
  transfers between devices with their start and end apart: 9 -> 8, of which waited for: 4 -> 5; matrix products, arithmetic and copies ran while one was open for 1% -> 1% of each run, Pallas kernels for 12% -> 12%
where the time goes in v3:
time: 98.3 us; the launch traced here: 97.6 us
  starting transfers between devices  33.5 us (34%)
  blocking collectives  22.6 us (23%)
  waiting for transfers between devices  20.2 us (21%)
  Pallas kernels  16.1 us (16%)
  local copies, waits for them, and re-layouts  3.86 us (4%)
    all_to_all x1, blocking collectives, local(): lax.all_to_all(placed, 'ctx', split_axis=0, concat_axis=0, tiled=True)  22.6 us
    all_to_all x3, starting transfers between devices, to_heads(): lax.all_to_all(value, 'head', split_axis=0, concat_axis=0, tiled=True)  20.9 us
    ppermute x1, waiting for transfers between devices, local(): lax.ppermute(own[:, :2 * frames].reshape(2 * block, HEAD_SIZE), 'ctx', ring)  8.79 us
    pallas_call x2, Pallas kernels, attend(): pl.pallas_call(functools.partial(main_kernel, scale, first_tile, tiles),...  7.27 us
    ppermute x1, waiting for transfers between devices, local(): before = lax.ppermute(told, 'ctx', ring)  6.95 us
    all_to_all x1, starting transfers between devices, local(): lax.all_to_all(after(shares, queries_here), 'head', split_axis=0, concat_...  3.41 us
    ppermute x1, starting transfers between devices, local(): came = lax.ppermute(send, 'head', pairs)  3.37 us
    pallas_call x1, Pallas kernels, local(): pl.pallas_call(functools.partial(pack_kernel, group), out_shape=shape_of(...  3.13 us
  transfers between devices with their start and end apart: 8, of which 5 were waited for; matrix products, arithmetic and copies ran while one was open for 1% of the time, Pallas kernels for 12%

profile of v3, /device:TPU:1, one launch (start us, length us, event | category | flops | bytes accessed | tf_op | source)
XLA Modules:
  0.0 97.6 jit_solution(10435327233975780158)
XLA Ops:
  0.6 3.1 %shard_map.113 = bf16[8,288,128]{2,1,0:T(8,128)(2,1)} custom-call(s32[64]{0:T(128)} %rows_ref.2, bf16[128,1024]{1,0:T(8,128)(2,1)} %keys_hbm.1, bf16[128,1024]{1,0:T(8,128)(2,1)} %values_hbm.1, bf16[128,4096]{1,0:T(8,128)(2,1)} %queries_hbm.1), custom_call_target="tpu_custom_call" | custom-call | flops 8388608 | bytes 2097152 | tf_op jit(solution)/shard_map/pallas_call | solution.py:403
  3.8 0.0 copy-start.5
  3.8 0.0 copy-start.7
  3.8 10.5 %all-to-all-start = ((bf16[8,288,128]{2,1,0:T(8,128)(2,1)}), bf16[8,288,128]{2,1,0:T(8,128)(2,1)S(1)}, u32[]{:S(2)}, u32[]{:S(2)}) async-start(bf16[8,288,128]{2,1,0:T(8,128)(2,1)} %shard_map.113), calls=%async_computation | async-start | bytes 1179648 | tf_op jit(solution)/shard_map/all_to_all | solution.py:379
  14.3 0.7 copy-done.2
  14.9 0.0 copy-done.4
  15.0 0.7 shard_map.114
  15.6 1.9 %collective-permute-start = (f32[8,128]{1,0:T(8,128)S(1)}, f32[8,128]{1,0:T(8,128)S(1)}, u32[]{:S(2)}, u32[]{:S(2)}) collective-permute-start(f32[8,128]{1,0:T(8,128)S(1)} %get-tuple-element.30), channel_id=1, source_target_pairs={{0,8},{8,16},{16,24},{24,32},{32,40},{40,48},{48,56},{56,64},{64,7... | collective-permute-start | bytes 12296 | tf_op jit(solution)/shard_map/ppermute | solution.py:436
  17.6 1.1 %copy.18 = bf16[16,8,8,512]{3,2,0,1:T(8,128)(2,1)} copy(bf16[16,8,8,512]{3,2,1,0:T(8,128)(2,1)S(1)} %bitcast.22) | data formatting | bytes 2097152 | tf_op jit(solution)/shard_map/reshape | solution.py:437
  18.6 7.0 %collective-permute-done.before_ref = f32[8,128]{1,0:T(8,128)S(1)} collective-permute-done((f32[8,128]{1,0:T(8,128)S(1)}, f32[8,128]{1,0:T(8,128)S(1)}, u32[]{:S(2)}, u32[]{:S(2)}) %collective-permute-start) | collective-permute-done | bytes 4128 | tf_op jit(solution)/shard_map/ppermute | solution.py:436
  25.6 0.8 slice.3
  26.4 2.0 %collective-permute-start.1 = (bf16[2048,128]{1,0:T(8,128)(2,1)}, bf16[2048,128]{1,0:T(8,128)(2,1)S(1)}, u32[]{:S(2)}, u32[]{:S(2)}) collective-permute-start(bf16[2048,128]{1,0:T(8,128)(2,1)} %bitcast.4), channel_id=1, source_target_pairs={{0,8},{8,16},{16,24},{24,32},{32,40},{40,48},{48,56},{56,64},{64,7... | collective-permute-start | bytes 1572872 | tf_op jit(solution)/shard_map/ppermute | solution.py:439
  28.5 5.7 %all-to-all-start.1 = ((bf16[8,128,512]{2,1,0:T(8,128)(2,1)}), bf16[8,128,512]{2,1,0:T(8,128)(2,1)}, u32[]{:S(2)}, u32[]{:S(2)}) async-start(bf16[8,128,512]{2,1,0:T(8,128)(2,1)} %bitcast.16), calls=%async_computation.1 | async-start | bytes 2097152 | tf_op jit(solution)/shard_map/all_to_all | solution.py:379
  34.2 1.9 %collective-permute-start.3 = (bf16[2,1024,256]{2,1,0:T(8,128)(2,1)S(1)}, bf16[2,1024,256]{2,1,0:T(8,128)(2,1)S(1)}, u32[]{:S(2)}, u32[]{:S(2)}) collective-permute-start(bf16[2,1024,256]{2,1,0:T(8,128)(2,1)S(1)} %copy-done), channel_id=1, source_target_pairs={{0,1},{1,0},{2,3},{3,2},{4,5},{5,4},{6,7},{7,6},{8,9},{9,8},{10,11... | collective-permute-start | bytes 3145736 | tf_op jit(solution)/shard_map/ppermute | solution.py:442
  36.1 1.1 %shard_map.115 = (f32[16,128]{1,0:T(8,128)S(1)}, s32[4]{0:T(128)S(1)}) custom-call(f32[8,128]{1,0:T(8,128)S(1)} %collective-permute-done.before_ref, f32[8,128]{1,0:T(8,128)S(1)} %get-tuple-element.34.docs_ref), custom_call_target="tpu_custom_call" | custom-call | bytes 131072 | tf_op jit(solution)/shard_map/pallas_call | solution.py:444
  37.2 8.8 %collective-permute-done.1.halo_ref = bf16[2048,128]{1,0:T(8,128)(2,1)S(1)} collective-permute-done((bf16[2048,128]{1,0:T(8,128)(2,1)}, bf16[2048,128]{1,0:T(8,128)(2,1)S(1)}, u32[]{:S(2)}, u32[]{:S(2)}) %collective-permute-start.1) | collective-permute-done | bytes 524320 | tf_op jit(solution)/shard_map/ppermute | solution.py:439
  46.0 1.2 %copy-done.6 = bf16[512,1024]{1,0:T(8,128)(2,1)S(1)} copy-done((bf16[512,1024]{1,0:T(8,128)(2,1)S(1)}, bf16[512,1024]{1,0:T(8,128)(2,1)}, u32[]{:S(2)}) %copy-start.6) | copy-done | bytes 1048600
  47.2 1.5 %shard_map.116 = (f32[32,1024]{1,0:T(8,128)S(1)}, bf16[32,1024]{1,0:T(8,128)(2,1)S(1)}) custom-call(bf16[8,288,128]{2,1,0:T(8,128)(2,1)S(1)} %all-to-all-done.own_ref, bf16[2048,128]{1,0:T(8,128)(2,1)S(1)} %collective-permute-done.1.halo_ref, f32[8,128]{1,0:T(8,128)S(1)} %collective-permute-done.before_ref, f32[8,128]{1,0:T(8,128)S(1)} %get-tuple-element.34.docs_ref, ...), custom_call_target="tpu_custom_call" | custom-call | flops 16106127360 | bytes 4194304 | tf_op jit(solution)/shard_map/pallas_call | solution.py:456
  48.8 3.4 %collective-permute-start.2 = (bf16[32,1024]{1,0:T(8,128)(2,1)S(1)}, bf16[32,1024]{1,0:T(8,128)(2,1)S(1)}, u32[]{:S(2)}, u32[]{:S(2)}) collective-permute-start(bf16[32,1024]{1,0:T(8,128)(2,1)S(1)} %get-tuple-element.40), channel_id=1, source_target_pairs={{0,1},{1,0},{2,3},{3,2},{4,5},{5,4},{6,7},{7,6},{8,9},{9,8},{10,11... | collective-permute-start | bytes 196616 | tf_op jit(solution)/shard_map/ppermute | solution.py:467
  52.2 0.9 collective-permute-done.2.came_ref
  53.0 0.7 shard_map.117
  53.8 3.4 %all-to-all-start.2 = ((bf16[4,32,1024]{2,1,0:T(8,128)(2,1)}), bf16[4,32,1024]{2,1,0:T(8,128)(2,1)S(1)}, u32[]{:S(2)}, u32[]{:S(2)}) async-start(bf16[4,32,1024]{2,1,0:T(8,128)(2,1)} %shard_map.117), calls=%async_computation.2 | async-start | bytes 524288 | tf_op jit(solution)/shard_map/all_to_all | solution.py:477
  57.2 0.0 copy-start.1
  57.2 3.3 %shard_map.118.refs_0_ = bf16[1024,512]{1,0:T(8,128)(2,1)} custom-call(s32[4]{0:T(128)S(1)} %get-tuple-element.48.low_ref, bf16[1024,512]{1,0:T(8,128)(2,1)} %bitcast.5.queries_ref, bf16[8,288,128]{2,1,0:T(8,128)(2,1)S(1)} %all-to-all-done.own_ref, bf16[2048,128]{1,0:T(8,128)(2,1)S(1)} %collective-permute-done.1.halo_ref, ...), custom_call_target="tpu_custom_call" | custom-call | flops 1610612736 | bytes 2097152 | tf_op jit(solution)/shard_map/pallas_call | solution.py:360
  60.5 2.8 %all-to-all-done.2.parts_ref = bf16[4,32,1024]{2,1,0:T(8,128)(2,1)S(1)} async-done(((bf16[4,32,1024]{2,1,0:T(8,128)(2,1)}), bf16[4,32,1024]{2,1,0:T(8,128)(2,1)S(1)}, u32[]{:S(2)}, u32[]{:S(2)}) %all-to-all-start.2) | async-done | bytes 262176 | tf_op jit(solution)/shard_map/all_to_all | solution.py:477
  63.3 1.4 %shard_map.119 = f32[8,8,128]{2,1,0:T(8,128)} custom-call(bf16[4,32,1024]{2,1,0:T(8,128)(2,1)S(1)} %all-to-all-done.2.parts_ref, f32[1,1024]{1,0:T(1,128)S(1)} %bitcast.18, bf16[2,1024,256]{2,1,0:T(8,128)(2,1)S(1)} %copy-done, bf16[2,1024,256]{2,1,0:T(8,128)(2,1)S(1)} %collective-permute-done.3.other_ref, f32[8,128]{1,0:T(8,128)S(1)} %get-tuple-element.47.info_ref), custom_call_target="tpu_custom_call" | custom-call | flops 134217728 | bytes 2097152 | tf_op jit(solution)/shard_map/pallas_call | solution.py:491
  64.7 4.7 %all-to-all-start.3 = ((f32[8,8,128]{2,1,0:T(8,128)}), f32[8,8,128]{2,1,0:T(8,128)S(1)}, u32[]{:S(2)}, u32[]{:S(2)}) async-start(f32[8,8,128]{2,1,0:T(8,128)} %shard_map.119), calls=%async_computation.3 | async-start | bytes 65536 | tf_op jit(solution)/shard_map/all_to_all | solution.py:379
  69.4 4.0 %shard_map.120 = bf16[1024,512]{1,0:T(8,128)(2,1)} custom-call(s32[4]{0:T(128)S(1)} %get-tuple-element.48.low_ref, bf16[1024,512]{1,0:T(8,128)(2,1)} %bitcast.5.queries_ref, bf16[8,288,128]{2,1,0:T(8,128)(2,1)S(1)} %all-to-all-done.own_ref, bf16[2048,128]{1,0:T(8,128)(2,1)S(1)} %collective-permute-done.1.halo_ref, ...), custom_call_target="tpu_custom_call", output_to_operand_aliasing={{}: (5, {})} | custom-call | flops 1610612736 | bytes 2097152 | tf_op jit(solution)/shard_map/pallas_call | solution.py:360
  73.4 0.7 all-to-all-done.3.stats_ref
  74.1 0.3 shard_map.121
  74.4 22.6 %all_to_all.29 = f32[64,1,128]{2,1,0:T(1,128)S(1)} all-to-all(f32[64,1,128]{2,1,0:T(1,128)S(1)} %bitcast.17), channel_id=1, replica_groups=mesh['ctx'=64,'head'=8] {'ctx'}, dimensions={0} | all-to-all | bytes 65536 | tf_op jit(solution)/shard_map/all_to_all | solution.py:521
  97.0 0.6 reduce_sum.9
  (13 shorter events, 0.0 us)
Async XLA Ops:
  3.8 10.5 %copy-start.5 = (s32[64,1]{0,1:T(1,128)S(1)}, s32[64,1]{0,1:T(1,128)}, u32[]{:S(2)}) copy-start(s32[64,1]{0,1:T(1,128)} %param.15) | copy-start | bytes 772
  3.8 13.8 %copy-start.7 = (bf16[128,4096]{1,0:T(8,128)(2,1)S(1)}, bf16[128,4096]{1,0:T(8,128)(2,1)}, u32[]{:S(2)}) copy-start(bf16[128,4096]{1,0:T(8,128)(2,1)} %queries_hbm.1) | copy-start | bytes 3145732
  3.8 21.8 %all-to-all-start = ((bf16[8,288,128]{2,1,0:T(8,128)(2,1)}), bf16[8,288,128]{2,1,0:T(8,128)(2,1)S(1)}, u32[]{:S(2)}, u32[]{:S(2)}) async-start(bf16[8,288,128]{2,1,0:T(8,128)(2,1)} %shard_map.113), calls=%async_computation | async-start | bytes 1179648 | tf_op jit(solution)/shard_map/all_to_all | solution.py:379
  14.3 0.7 copy-start.2
  14.3 0.7 copy-start.3
  14.3 0.7 copy-start.4
  15.6 10.0 %collective-permute-start = (f32[8,128]{1,0:T(8,128)S(1)}, f32[8,128]{1,0:T(8,128)S(1)}, u32[]{:S(2)}, u32[]{:S(2)}) collective-permute-start(f32[8,128]{1,0:T(8,128)S(1)} %get-tuple-element.30), channel_id=1, source_target_pairs={{0,8},{8,16},{16,24},{24,32},{32,40},{40,48},{48,56},{56,64},{64,7... | collective-permute-start | bytes 12296 | tf_op jit(solution)/shard_map/ppermute | solution.py:436
  26.4 7.7 %copy-start = (bf16[2,1024,256]{2,1,0:T(8,128)(2,1)S(1)}, bf16[2,1024,256]{2,1,0:T(8,128)(2,1)}, u32[]{:S(2)}) copy-start(bf16[2,1024,256]{2,1,0:T(8,128)(2,1)} %codes_ref.1) | copy-start | bytes 3145732
  26.4 19.6 %collective-permute-start.1 = (bf16[2048,128]{1,0:T(8,128)(2,1)}, bf16[2048,128]{1,0:T(8,128)(2,1)S(1)}, u32[]{:S(2)}, u32[]{:S(2)}) collective-permute-start(bf16[2048,128]{1,0:T(8,128)(2,1)} %bitcast.4), channel_id=1, source_target_pairs={{0,8},{8,16},{16,24},{24,32},{32,40},{40,48},{48,56},{56,64},{64,7... | collective-permute-start | bytes 1572872 | tf_op jit(solution)/shard_map/ppermute | solution.py:439
  28.5 25.3 %all-to-all-start.1 = ((bf16[8,128,512]{2,1,0:T(8,128)(2,1)}), bf16[8,128,512]{2,1,0:T(8,128)(2,1)}, u32[]{:S(2)}, u32[]{:S(2)}) async-start(bf16[8,128,512]{2,1,0:T(8,128)(2,1)} %bitcast.16), calls=%async_computation.1 | async-start | bytes 2097152 | tf_op jit(solution)/shard_map/all_to_all | solution.py:379
  34.2 29.1 %collective-permute-start.3 = (bf16[2,1024,256]{2,1,0:T(8,128)(2,1)S(1)}, bf16[2,1024,256]{2,1,0:T(8,128)(2,1)S(1)}, u32[]{:S(2)}, u32[]{:S(2)}) collective-permute-start(bf16[2,1024,256]{2,1,0:T(8,128)(2,1)S(1)} %copy-done), channel_id=1, source_target_pairs={{0,1},{1,0},{2,3},{3,2},{4,5},{5,4},{6,7},{7,6},{8,9},{9,8},{10,11... | collective-permute-start | bytes 3145736 | tf_op jit(solution)/shard_map/ppermute | solution.py:442
  46.0 1.2 %copy-start.6 = (bf16[512,1024]{1,0:T(8,128)(2,1)S(1)}, bf16[512,1024]{1,0:T(8,128)(2,1)}, u32[]{:S(2)}) copy-start(bf16[512,1024]{1,0:T(8,128)(2,1)} %proj_ref.1) | copy-start | bytes 3145732
  48.8 4.3 %collective-permute-start.2 = (bf16[32,1024]{1,0:T(8,128)(2,1)S(1)}, bf16[32,1024]{1,0:T(8,128)(2,1)S(1)}, u32[]{:S(2)}, u32[]{:S(2)}) collective-permute-start(bf16[32,1024]{1,0:T(8,128)(2,1)S(1)} %get-tuple-element.40), channel_id=1, source_target_pairs={{0,1},{1,0},{2,3},{3,2},{4,5},{5,4},{6,7},{7,6},{8,9},{9,8},{10,11... | collective-permute-start | bytes 196616 | tf_op jit(solution)/shard_map/ppermute | solution.py:467
  53.8 9.5 %all-to-all-start.2 = ((bf16[4,32,1024]{2,1,0:T(8,128)(2,1)}), bf16[4,32,1024]{2,1,0:T(8,128)(2,1)S(1)}, u32[]{:S(2)}, u32[]{:S(2)}) async-start(bf16[4,32,1024]{2,1,0:T(8,128)(2,1)} %shard_map.117), calls=%async_computation.2 | async-start | bytes 524288 | tf_op jit(solution)/shard_map/all_to_all | solution.py:477
  57.2 6.1 %copy-start.1 = (f32[1024]{0:T(1024)S(1)}, f32[1024]{0:T(1024)}, u32[]{:S(2)}) copy-start(f32[1024]{0:T(1024)} %param.18) | copy-start | bytes 12292
  64.7 9.5 %all-to-all-start.3 = ((f32[8,8,128]{2,1,0:T(8,128)}), f32[8,8,128]{2,1,0:T(8,128)S(1)}, u32[]{:S(2)}, u32[]{:S(2)}) async-start(f32[8,8,128]{2,1,0:T(8,128)} %shard_map.119), calls=%async_computation.3 | async-start | bytes 65536 | tf_op jit(solution)/shard_map/all_to_all | solution.py:379

commit v4 on v3

--- a/solution.py
+++ b/solution.py
@@ -121,13 +121,16 @@
     return halo_ref[pl.ds((2 * s + which) * frames, frames), :]
 
 
-def window_kernel(before_ref, docs_ref, all_docs_ref, low_ref):
+def window_kernel(before_ref, docs_ref, proj_hbm, all_docs_ref, low_ref, proj_ref, sem):
+    fetch = pltpu.make_async_copy(proj_hbm, proj_ref, sem)
+    fetch.start()
     docs = jnp.concatenate([before_ref[...], docs_ref[...]], axis=0)
     all_docs_ref[...] = docs
     for t in range(low_ref.shape[0]):
         first = docs_ref[t * QUERY_TILE // HEAD_SIZE : t * QUERY_TILE // HEAD_SIZE + 1, 0:1]
         below = jnp.where(docs < first, 1.0, 0.0)
         low_ref[t] = jnp.sum(below).astype(jnp.int32) // KEY_TILE
+    fetch.wait()
 
 
 def sample_kernel(
@@ -441,18 +444,20 @@
     pairs = [(s, s + 1 - 2 * (s % 2)) for s in range(heads)]
     other_codes = lax.ppermute(after(code_heads, own), "head", pairs)
 
-    across, low = pl.pallas_call(
+    across, low, proj_here = pl.pallas_call(
         window_kernel,
         out_shape=(
             shape_of((2 * heads, frames), f32),
             shape_of((block // QUERY_TILE,), jnp.int32),
+            shape_of(in_proj.shape, bf16),
         ),
-        in_specs=[VMEM] * 2,
-        out_specs=(VMEM, SMEM),
+        in_specs=[VMEM, VMEM, ANY],
+        out_specs=(VMEM, SMEM, VMEM),
+        scratch_shapes=[pltpu.SemaphoreType.DMA],
         compiler_params=params(8),
         cost_estimate=cost(0, 2 * 2**16),
-    )(before, docs)
-    halo, across, low = lax.optimization_barrier((halo, across, low))
+    )(before, docs, after(in_proj, own))
+    halo, across, low, proj_here = lax.optimization_barrier((halo, across, low, proj_here))
     keep, send = pl.pallas_call(
         functools.partial(sample_kernel, scale),
         out_shape=(shape_of((samples // 2, deep), f32), shape_of((samples // 2, deep), bf16)),
@@ -463,7 +468,7 @@
         cost_estimate=cost(
             240 * samples * group * 2 * block * HEAD_SIZE, 4 * 2**20, samples * group * 2 * block
         ),
-    )(own, halo, before, docs, mine, in_proj)
+    )(own, halo, before, docs, mine, proj_here)
     came = lax.ppermute(send, "head", pairs)
 
     shares = pl.pallas_call(

time: 98.3 us -> 97.7 us (level)
  waiting for transfers between devices: 20.2 us -> 18.2 us
    ppermute x1, waiting for transfers between devices: 8.79 us -> 7.49 us  [local(): lax.ppermute(own[:, :2 * frames].reshape(2 * block, HEAD_SIZE), 'ctx', ring)]
  transfers between devices with their start and end apart: 8 -> 8, of which waited for: 5 -> 4; matrix products, arithmetic and copies ran while one was open for 1% -> 1% of each run, Pallas kernels for 12% -> 13%
where the time goes in v4:
time: 97.7 us; the launch traced here: 96.8 us
  starting transfers between devices  33.5 us (34%)
  blocking collectives  23 us (24%)
  waiting for transfers between devices  18.2 us (19%)
  Pallas kernels  16.9 us (17%)
  local copies, waits for them, and re-layouts  3.85 us (4%)
    all_to_all x1, blocking collectives, local(): lax.all_to_all(placed, 'ctx', split_axis=0, concat_axis=0, tiled=True)  23 us
    all_to_all x3, starting transfers between devices, to_heads(): lax.all_to_all(value, 'head', split_axis=0, concat_axis=0, tiled=True)  20.9 us
    pallas_call x2, Pallas kernels, attend(): pl.pallas_call(functools.partial(main_kernel, scale, first_tile, tiles),...  8.05 us
    ppermute x1, waiting for transfers between devices, local(): lax.ppermute(own[:, :2 * frames].reshape(2 * block, HEAD_SIZE), 'ctx', ring)  7.49 us
    ppermute x1, waiting for transfers between devices, local(): before = lax.ppermute(told, 'ctx', ring)  6.95 us
    all_to_all x1, starting transfers between devices, local(): lax.all_to_all(after(shares, queries_here), 'head', split_axis=0, concat_...  3.41 us
    ppermute x1, starting transfers between devices, local(): came = lax.ppermute(send, 'head', pairs)  3.35 us
    pallas_call x1, Pallas kernels, local(): pl.pallas_call(functools.partial(pack_kernel, group), out_shape=shape_of(...  3.13 us
  transfers between devices with their start and end apart: 8, of which 4 were waited for; matrix products, arithmetic and copies ran while one was open for 1% of the time, Pallas kernels for 13%

profile of v4, /device:TPU:1, one launch (start us, length us, event | category | flops | bytes accessed | tf_op | source)
XLA Modules:
  0.0 96.8 jit_solution(13154602282407644600)
XLA Ops:
  0.6 3.1 %shard_map.113 = bf16[8,288,128]{2,1,0:T(8,128)(2,1)} custom-call(s32[64]{0:T(128)} %rows_ref.2, bf16[128,1024]{1,0:T(8,128)(2,1)} %keys_hbm.1, bf16[128,1024]{1,0:T(8,128)(2,1)} %values_hbm.1, bf16[128,4096]{1,0:T(8,128)(2,1)} %queries_hbm.1), custom_call_target="tpu_custom_call" | custom-call | flops 8388608 | bytes 2097152 | tf_op jit(solution)/shard_map/pallas_call | solution.py:406
  3.8 0.0 copy-start.6
  3.8 0.0 copy-start.7
  3.8 10.5 %all-to-all-start = ((bf16[8,288,128]{2,1,0:T(8,128)(2,1)}), bf16[8,288,128]{2,1,0:T(8,128)(2,1)S(1)}, u32[]{:S(2)}, u32[]{:S(2)}) async-start(bf16[8,288,128]{2,1,0:T(8,128)(2,1)} %shard_map.113), calls=%async_computation | async-start | bytes 1179648 | tf_op jit(solution)/shard_map/all_to_all | solution.py:382
  14.3 0.7 copy-done.3
  14.9 0.0 copy-done.5
  15.0 0.7 shard_map.114
  15.6 1.9 %collective-permute-start = (f32[8,128]{1,0:T(8,128)S(1)}, f32[8,128]{1,0:T(8,128)S(1)}, u32[]{:S(2)}, u32[]{:S(2)}) collective-permute-start(f32[8,128]{1,0:T(8,128)S(1)} %get-tuple-element.33), channel_id=1, source_target_pairs={{0,8},{8,16},{16,24},{24,32},{32,40},{40,48},{48,56},{56,64},{64,7... | collective-permute-start | bytes 12296 | tf_op jit(solution)/shard_map/ppermute | solution.py:439
  17.6 1.1 %copy.18 = bf16[16,8,8,512]{3,2,0,1:T(8,128)(2,1)} copy(bf16[16,8,8,512]{3,2,1,0:T(8,128)(2,1)S(1)} %bitcast.22) | data formatting | bytes 2097152 | tf_op jit(solution)/shard_map/reshape | solution.py:440
  18.6 7.0 %collective-permute-done.before_ref = f32[8,128]{1,0:T(8,128)S(1)} collective-permute-done((f32[8,128]{1,0:T(8,128)S(1)}, f32[8,128]{1,0:T(8,128)S(1)}, u32[]{:S(2)}, u32[]{:S(2)}) %collective-permute-start) | collective-permute-done | bytes 4128 | tf_op jit(solution)/shard_map/ppermute | solution.py:439
  25.6 0.8 slice.3
  26.4 2.0 %collective-permute-start.1 = (bf16[2048,128]{1,0:T(8,128)(2,1)}, bf16[2048,128]{1,0:T(8,128)(2,1)S(1)}, u32[]{:S(2)}, u32[]{:S(2)}) collective-permute-start(bf16[2048,128]{1,0:T(8,128)(2,1)} %bitcast.4), channel_id=1, source_target_pairs={{0,8},{8,16},{16,24},{24,32},{32,40},{40,48},{48,56},{56,64},{64,7... | collective-permute-start | bytes 1572872 | tf_op jit(solution)/shard_map/ppermute | solution.py:442
  28.5 5.7 %all-to-all-start.1 = ((bf16[8,128,512]{2,1,0:T(8,128)(2,1)}), bf16[8,128,512]{2,1,0:T(8,128)(2,1)}, u32[]{:S(2)}, u32[]{:S(2)}) async-start(bf16[8,128,512]{2,1,0:T(8,128)(2,1)} %bitcast.16), calls=%async_computation.1 | async-start | bytes 2097152 | tf_op jit(solution)/shard_map/all_to_all | solution.py:382
  34.2 1.9 %collective-permute-start.3 = (bf16[2,1024,256]{2,1,0:T(8,128)(2,1)S(1)}, bf16[2,1024,256]{2,1,0:T(8,128)(2,1)S(1)}, u32[]{:S(2)}, u32[]{:S(2)}) collective-permute-start(bf16[2,1024,256]{2,1,0:T(8,128)(2,1)S(1)} %copy-done), channel_id=1, source_target_pairs={{0,1},{1,0},{2,3},{3,2},{4,5},{5,4},{6,7},{7,6},{8,9},{9,8},{10,11... | collective-permute-start | bytes 3145736 | tf_op jit(solution)/shard_map/ppermute | solution.py:445
  36.1 0.0 copy-start.1
  36.1 1.2 %copy-done.1 = bf16[512,1024]{1,0:T(8,128)(2,1)S(1)} copy-done((bf16[512,1024]{1,0:T(8,128)(2,1)S(1)}, bf16[512,1024]{1,0:T(8,128)(2,1)}, u32[]{:S(2)}) %copy-start.1) | copy-done | bytes 1048600
  37.3 1.2 %shard_map.115 = (f32[16,128]{1,0:T(8,128)S(1)}, s32[4]{0:T(128)S(1)}, bf16[512,1024]{1,0:T(8,128)(2,1)S(1)}) custom-call(f32[8,128]{1,0:T(8,128)S(1)} %collective-permute-done.before_ref, f32[8,128]{1,0:T(8,128)S(1)} %get-tuple-element.37.docs_ref, bf16[512,1024]{1,0:T(8,128)(2,1)S(1)} %copy-done.1), custom_call_target="tpu_custom_call" | custom-call | bytes 131072 | tf_op jit(solution)/shard_map/pallas_call | solution.py:447
  38.5 7.5 %collective-permute-done.1.halo_ref = bf16[2048,128]{1,0:T(8,128)(2,1)S(1)} collective-permute-done((bf16[2048,128]{1,0:T(8,128)(2,1)}, bf16[2048,128]{1,0:T(8,128)(2,1)S(1)}, u32[]{:S(2)}, u32[]{:S(2)}) %collective-permute-start.1) | collective-permute-done | bytes 524320 | tf_op jit(solution)/shard_map/ppermute | solution.py:442
  46.0 1.5 %shard_map.116 = (f32[32,1024]{1,0:T(8,128)S(1)}, bf16[32,1024]{1,0:T(8,128)(2,1)S(1)}) custom-call(bf16[8,288,128]{2,1,0:T(8,128)(2,1)S(1)} %all-to-all-done.own_ref, bf16[2048,128]{1,0:T(8,128)(2,1)S(1)} %collective-permute-done.1.halo_ref, f32[8,128]{1,0:T(8,128)S(1)} %collective-permute-done.before_ref, f32[8,128]{1,0:T(8,128)S(1)} %get-tuple-element.37.docs_ref, ...), custom_call_target="tpu_custom_call" | custom-call | flops 16106127360 | bytes 4194304 | tf_op jit(solution)/shard_map/pallas_call | solution.py:461
  47.6 3.4 %collective-permute-start.2 = (bf16[32,1024]{1,0:T(8,128)(2,1)S(1)}, bf16[32,1024]{1,0:T(8,128)(2,1)S(1)}, u32[]{:S(2)}, u32[]{:S(2)}) collective-permute-start(bf16[32,1024]{1,0:T(8,128)(2,1)S(1)} %get-tuple-element.46), channel_id=1, source_target_pairs={{0,1},{1,0},{2,3},{3,2},{4,5},{5,4},{6,7},{7,6},{8,9},{9,8},{10,11... | collective-permute-start | bytes 196616 | tf_op jit(solution)/shard_map/ppermute | solution.py:472
  50.9 0.9 collective-permute-done.2.came_ref
  51.8 0.7 shard_map.117
  52.5 3.4 %all-to-all-start.2 = ((bf16[4,32,1024]{2,1,0:T(8,128)(2,1)}), bf16[4,32,1024]{2,1,0:T(8,128)(2,1)S(1)}, u32[]{:S(2)}, u32[]{:S(2)}) async-start(bf16[4,32,1024]{2,1,0:T(8,128)(2,1)} %shard_map.117), calls=%async_computation.2 | async-start | bytes 524288 | tf_op jit(solution)/shard_map/all_to_all | solution.py:482
  56.0 0.0 copy-start.2
  56.0 3.3 %shard_map.118.refs_0_ = bf16[1024,512]{1,0:T(8,128)(2,1)} custom-call(s32[4]{0:T(128)S(1)} %get-tuple-element.54.low_ref, bf16[1024,512]{1,0:T(8,128)(2,1)} %bitcast.5.queries_ref, bf16[8,288,128]{2,1,0:T(8,128)(2,1)S(1)} %all-to-all-done.own_ref, bf16[2048,128]{1,0:T(8,128)(2,1)S(1)} %collective-permute-done.1.halo_ref, ...), custom_call_target="tpu_custom_call" | custom-call | flops 1610612736 | bytes 2097152 | tf_op jit(solution)/shard_map/pallas_call | solution.py:363
  59.2 2.8 %all-to-all-done.2.parts_ref = bf16[4,32,1024]{2,1,0:T(8,128)(2,1)S(1)} async-done(((bf16[4,32,1024]{2,1,0:T(8,128)(2,1)}), bf16[4,32,1024]{2,1,0:T(8,128)(2,1)S(1)}, u32[]{:S(2)}, u32[]{:S(2)}) %all-to-all-start.2) | async-done | bytes 262176 | tf_op jit(solution)/shard_map/all_to_all | solution.py:482
  62.1 1.4 %shard_map.119 = f32[8,8,128]{2,1,0:T(8,128)} custom-call(bf16[4,32,1024]{2,1,0:T(8,128)(2,1)S(1)} %all-to-all-done.2.parts_ref, f32[1,1024]{1,0:T(1,128)S(1)} %bitcast.18, bf16[2,1024,256]{2,1,0:T(8,128)(2,1)S(1)} %copy-done, bf16[2,1024,256]{2,1,0:T(8,128)(2,1)S(1)} %collective-permute-done.3.other_ref, f32[8,128]{1,0:T(8,128)S(1)} %get-tuple-element.53.info_ref), custom_call_target="tpu_custom_call" | custom-call | flops 134217728 | bytes 2097152 | tf_op jit(solution)/shard_map/pallas_call | solution.py:496
  63.4 4.7 %all-to-all-start.3 = ((f32[8,8,128]{2,1,0:T(8,128)}), f32[8,8,128]{2,1,0:T(8,128)S(1)}, u32[]{:S(2)}, u32[]{:S(2)}) async-start(f32[8,8,128]{2,1,0:T(8,128)} %shard_map.119), calls=%async_computation.3 | async-start | bytes 65536 | tf_op jit(solution)/shard_map/all_to_all | solution.py:382
  68.2 4.8 %shard_map.120 = bf16[1024,512]{1,0:T(8,128)(2,1)} custom-call(s32[4]{0:T(128)S(1)} %get-tuple-element.54.low_ref, bf16[1024,512]{1,0:T(8,128)(2,1)} %bitcast.5.queries_ref, bf16[8,288,128]{2,1,0:T(8,128)(2,1)S(1)} %all-to-all-done.own_ref, bf16[2048,128]{1,0:T(8,128)(2,1)S(1)} %collective-permute-done.1.halo_ref, ...), custom_call_target="tpu_custom_call", output_to_operand_aliasing={{}: (5, {})} | custom-call | flops 1610612736 | bytes 2097152 | tf_op jit(solution)/shard_map/pallas_call | solution.py:363
  73.0 0.3 shard_map.121
  73.2 23.0 %all_to_all.29 = f32[64,1,128]{2,1,0:T(1,128)S(1)} all-to-all(f32[64,1,128]{2,1,0:T(1,128)S(1)} %bitcast.17), channel_id=1, replica_groups=mesh['ctx'=64,'head'=8] {'ctx'}, dimensions={0} | all-to-all | bytes 65536 | tf_op jit(solution)/shard_map/all_to_all | solution.py:526
  96.2 0.6 reduce_sum.9
  (13 shorter events, 0.0 us)
Async XLA Ops:
  3.8 10.5 %copy-start.6 = (s32[64,1]{0,1:T(1,128)S(1)}, s32[64,1]{0,1:T(1,128)}, u32[]{:S(2)}) copy-start(s32[64,1]{0,1:T(1,128)} %param.15) | copy-start | bytes 772
  3.8 13.8 %copy-start.7 = (bf16[128,4096]{1,0:T(8,128)(2,1)S(1)}, bf16[128,4096]{1,0:T(8,128)(2,1)}, u32[]{:S(2)}) copy-start(bf16[128,4096]{1,0:T(8,128)(2,1)} %queries_hbm.1) | copy-start | bytes 3145732
  3.8 21.8 %all-to-all-start = ((bf16[8,288,128]{2,1,0:T(8,128)(2,1)}), bf16[8,288,128]{2,1,0:T(8,128)(2,1)S(1)}, u32[]{:S(2)}, u32[]{:S(2)}) async-start(bf16[8,288,128]{2,1,0:T(8,128)(2,1)} %shard_map.113), calls=%async_computation | async-start | bytes 1179648 | tf_op jit(solution)/shard_map/all_to_all | solution.py:382
  14.3 0.7 copy-start.3
  14.3 0.7 copy-start.4
  14.3 0.7 copy-start.5
  15.6 10.0 %collective-permute-start = (f32[8,128]{1,0:T(8,128)S(1)}, f32[8,128]{1,0:T(8,128)S(1)}, u32[]{:S(2)}, u32[]{:S(2)}) collective-permute-start(f32[8,128]{1,0:T(8,128)S(1)} %get-tuple-element.33), channel_id=1, source_target_pairs={{0,8},{8,16},{16,24},{24,32},{32,40},{40,48},{48,56},{56,64},{64,7... | collective-permute-start | bytes 12296 | tf_op jit(solution)/shard_map/ppermute | solution.py:439
  26.4 7.7 %copy-start = (bf16[2,1024,256]{2,1,0:T(8,128)(2,1)S(1)}, bf16[2,1024,256]{2,1,0:T(8,128)(2,1)}, u32[]{:S(2)}) copy-start(bf16[2,1024,256]{2,1,0:T(8,128)(2,1)} %codes_ref.1) | copy-start | bytes 3145732
  26.4 19.6 %collective-permute-start.1 = (bf16[2048,128]{1,0:T(8,128)(2,1)}, bf16[2048,128]{1,0:T(8,128)(2,1)S(1)}, u32[]{:S(2)}, u32[]{:S(2)}) collective-permute-start(bf16[2048,128]{1,0:T(8,128)(2,1)} %bitcast.4), channel_id=1, source_target_pairs={{0,8},{8,16},{16,24},{24,32},{32,40},{40,48},{48,56},{56,64},{64,7... | collective-permute-start | bytes 1572872 | tf_op jit(solution)/shard_map/ppermute | solution.py:442
  28.5 24.1 %all-to-all-start.1 = ((bf16[8,128,512]{2,1,0:T(8,128)(2,1)}), bf16[8,128,512]{2,1,0:T(8,128)(2,1)}, u32[]{:S(2)}, u32[]{:S(2)}) async-start(bf16[8,128,512]{2,1,0:T(8,128)(2,1)} %bitcast.16), calls=%async_computation.1 | async-start | bytes 2097152 | tf_op jit(solution)/shard_map/all_to_all | solution.py:382
  34.2 27.9 %collective-permute-start.3 = (bf16[2,1024,256]{2,1,0:T(8,128)(2,1)S(1)}, bf16[2,1024,256]{2,1,0:T(8,128)(2,1)S(1)}, u32[]{:S(2)}, u32[]{:S(2)}) collective-permute-start(bf16[2,1024,256]{2,1,0:T(8,128)(2,1)S(1)} %copy-done), channel_id=1, source_target_pairs={{0,1},{1,0},{2,3},{3,2},{4,5},{5,4},{6,7},{7,6},{8,9},{9,8},{10,11... | collective-permute-start | bytes 3145736 | tf_op jit(solution)/shard_map/ppermute | solution.py:445
  36.1 1.2 %copy-start.1 = (bf16[512,1024]{1,0:T(8,128)(2,1)S(1)}, bf16[512,1024]{1,0:T(8,128)(2,1)}, u32[]{:S(2)}) copy-start(bf16[512,1024]{1,0:T(8,128)(2,1)} %proj_hbm) | copy-start | bytes 3145732
  47.6 4.2 %collective-permute-start.2 = (bf16[32,1024]{1,0:T(8,128)(2,1)S(1)}, bf16[32,1024]{1,0:T(8,128)(2,1)S(1)}, u32[]{:S(2)}, u32[]{:S(2)}) collective-permute-start(bf16[32,1024]{1,0:T(8,128)(2,1)S(1)} %get-tuple-element.46), channel_id=1, source_target_pairs={{0,1},{1,0},{2,3},{3,2},{4,5},{5,4},{6,7},{7,6},{8,9},{9,8},{10,11... | collective-permute-start | bytes 196616 | tf_op jit(solution)/shard_map/ppermute | solution.py:472
  52.5 9.5 %all-to-all-start.2 = ((bf16[4,32,1024]{2,1,0:T(8,128)(2,1)}), bf16[4,32,1024]{2,1,0:T(8,128)(2,1)S(1)}, u32[]{:S(2)}, u32[]{:S(2)}) async-start(bf16[4,32,1024]{2,1,0:T(8,128)(2,1)} %shard_map.117), calls=%async_computation.2 | async-start | bytes 524288 | tf_op jit(solution)/shard_map/all_to_all | solution.py:482
  56.0 6.1 %copy-start.2 = (f32[1024]{0:T(1024)S(1)}, f32[1024]{0:T(1024)}, u32[]{:S(2)}) copy-start(f32[1024]{0:T(1024)} %param.18) | copy-start | bytes 12292
  63.4 9.5 %all-to-all-start.3 = ((f32[8,8,128]{2,1,0:T(8,128)}), f32[8,8,128]{2,1,0:T(8,128)S(1)}, u32[]{:S(2)}, u32[]{:S(2)}) async-start(f32[8,8,128]{2,1,0:T(8,128)} %shard_map.119), calls=%async_computation.3 | async-start | bytes 65536 | tf_op jit(solution)/shard_map/all_to_all | solution.py:382

commit v5 on v4

--- a/solution.py
+++ b/solution.py
@@ -210,6 +210,10 @@
     me = lax.axis_index("head")
     odd = lax.rem(me, 2) == 1
     other = jnp.where(odd, me - 1, me + 1)
+    info = info_ref[...]
+    below = jnp.zeros((128 - info.shape[0], 128), f32)
+    down = jnp.transpose(jnp.concatenate([info, below], axis=0))
+    mine = jnp.where(odd, down[samples : 2 * samples], down[:samples])
     state = parts_ref[0].astype(f32)
     for s in range(1, count):
         state = state + parts_ref[s].astype(f32)
@@ -223,8 +227,7 @@
         second = jnp.dot(normed, other_ref[b], preferred_element_type=f32)
         top = jnp.max(jnp.maximum(first, second), axis=1, keepdims=True)
         mass = jnp.sum(jnp.exp(first - top) + jnp.exp(second - top), axis=1, keepdims=True)
-        column = turned(info_ref[2 + b : 3 + b, :])
-        wanted = jnp.where(odd, column[samples : 2 * samples], column[:samples])[:, 0:1]
+        wanted = mine[:, 2 + b : 3 + b]
         hit = jnp.where(code == wanted - (me * codes).astype(f32), first, 0.0)
         hit = hit + jnp.where(code == wanted - (other * codes).astype(f32), second, 0.0)
         target = jnp.sum(hit, axis=1, keepdims=True)

time: 97.7 us -> 98.1 us (level)
  no operation moved by 1% of the time
where the time goes in v5:
time: 98.1 us; the launch traced here: 96.9 us
  starting transfers between devices  33.5 us (34%)
  blocking collectives  23.1 us (24%)
  waiting for transfers between devices  18.2 us (19%)
  Pallas kernels  17 us (17%)
  local copies, waits for them, and re-layouts  3.85 us (4%)
    all_to_all x1, blocking collectives, local(): lax.all_to_all(placed, 'ctx', split_axis=0, concat_axis=0, tiled=True)  23.1 us
    all_to_all x3, starting transfers between devices, to_heads(): lax.all_to_all(value, 'head', split_axis=0, concat_axis=0, tiled=True)  20.9 us
    pallas_call x2, Pallas kernels, attend(): pl.pallas_call(functools.partial(main_kernel, scale, first_tile, tiles),...  8.06 us
    ppermute x1, waiting for transfers between devices, local(): lax.ppermute(own[:, :2 * frames].reshape(2 * block, HEAD_SIZE), 'ctx', ring)  7.49 us
    ppermute x1, waiting for transfers between devices, local(): before = lax.ppermute(told, 'ctx', ring)  6.95 us
    all_to_all x1, starting transfers between devices, local(): lax.all_to_all(after(shares, queries_here), 'head', split_axis=0, concat_...  3.41 us
    ppermute x1, starting transfers between devices, local(): came = lax.ppermute(send, 'head', pairs)  3.35 us
    pallas_call x1, Pallas kernels, local(): pl.pallas_call(functools.partial(pack_kernel, group), out_shape=shape_of(...  3.13 us
  transfers between devices with their start and end apart: 8, of which 4 were waited for; matrix products, arithmetic and copies ran while one was open for 1% of the time, Pallas kernels for 13%

profile of v5, /device:TPU:1, one launch (start us, length us, event | category | flops | bytes accessed | tf_op | source)
XLA Modules:
  0.0 96.9 jit_solution(12143176113666654224)
XLA Ops:
  0.6 3.1 %shard_map.113 = bf16[8,288,128]{2,1,0:T(8,128)(2,1)} custom-call(s32[64]{0:T(128)} %rows_ref.2, bf16[128,1024]{1,0:T(8,128)(2,1)} %keys_hbm.1, bf16[128,1024]{1,0:T(8,128)(2,1)} %values_hbm.1, bf16[128,4096]{1,0:T(8,128)(2,1)} %queries_hbm.1), custom_call_target="tpu_custom_call" | custom-call | flops 8388608 | bytes 2097152 | tf_op jit(solution)/shard_map/pallas_call | solution.py:409
  3.8 0.0 copy-start.6
  3.8 0.0 copy-start.7
  3.8 10.5 %all-to-all-start = ((bf16[8,288,128]{2,1,0:T(8,128)(2,1)}), bf16[8,288,128]{2,1,0:T(8,128)(2,1)S(1)}, u32[]{:S(2)}, u32[]{:S(2)}) async-start(bf16[8,288,128]{2,1,0:T(8,128)(2,1)} %shard_map.113), calls=%async_computation | async-start | bytes 1179648 | tf_op jit(solution)/shard_map/all_to_all | solution.py:385
  14.3 0.7 copy-done.3
  14.9 0.0 copy-done.5
  15.0 0.7 shard_map.114
  15.6 1.9 %collective-permute-start = (f32[8,128]{1,0:T(8,128)S(1)}, f32[8,128]{1,0:T(8,128)S(1)}, u32[]{:S(2)}, u32[]{:S(2)}) collective-permute-start(f32[8,128]{1,0:T(8,128)S(1)} %get-tuple-element.33), channel_id=1, source_target_pairs={{0,8},{8,16},{16,24},{24,32},{32,40},{40,48},{48,56},{56,64},{64,7... | collective-permute-start | bytes 12296 | tf_op jit(solution)/shard_map/ppermute | solution.py:442
  17.6 1.1 %copy.18 = bf16[16,8,8,512]{3,2,0,1:T(8,128)(2,1)} copy(bf16[16,8,8,512]{3,2,1,0:T(8,128)(2,1)S(1)} %bitcast.22) | data formatting | bytes 2097152 | tf_op jit(solution)/shard_map/reshape | solution.py:443
  18.6 7.0 %collective-permute-done.before_ref = f32[8,128]{1,0:T(8,128)S(1)} collective-permute-done((f32[8,128]{1,0:T(8,128)S(1)}, f32[8,128]{1,0:T(8,128)S(1)}, u32[]{:S(2)}, u32[]{:S(2)}) %collective-permute-start) | collective-permute-done | bytes 4128 | tf_op jit(solution)/shard_map/ppermute | solution.py:442
  25.6 0.8 slice.3
  26.4 2.0 %collective-permute-start.1 = (bf16[2048,128]{1,0:T(8,128)(2,1)}, bf16[2048,128]{1,0:T(8,128)(2,1)S(1)}, u32[]{:S(2)}, u32[]{:S(2)}) collective-permute-start(bf16[2048,128]{1,0:T(8,128)(2,1)} %bitcast.4), channel_id=1, source_target_pairs={{0,8},{8,16},{16,24},{24,32},{32,40},{40,48},{48,56},{56,64},{64,7... | collective-permute-start | bytes 1572872 | tf_op jit(solution)/shard_map/ppermute | solution.py:445
  28.5 5.7 %all-to-all-start.1 = ((bf16[8,128,512]{2,1,0:T(8,128)(2,1)}), bf16[8,128,512]{2,1,0:T(8,128)(2,1)}, u32[]{:S(2)}, u32[]{:S(2)}) async-start(bf16[8,128,512]{2,1,0:T(8,128)(2,1)} %bitcast.16), calls=%async_computation.1 | async-start | bytes 2097152 | tf_op jit(solution)/shard_map/all_to_all | solution.py:385
  34.2 1.9 %collective-permute-start.3 = (bf16[2,1024,256]{2,1,0:T(8,128)(2,1)S(1)}, bf16[2,1024,256]{2,1,0:T(8,128)(2,1)S(1)}, u32[]{:S(2)}, u32[]{:S(2)}) collective-permute-start(bf16[2,1024,256]{2,1,0:T(8,128)(2,1)S(1)} %copy-done), channel_id=1, source_target_pairs={{0,1},{1,0},{2,3},{3,2},{4,5},{5,4},{6,7},{7,6},{8,9},{9,8},{10,11... | collective-permute-start | bytes 3145736 | tf_op jit(solution)/shard_map/ppermute | solution.py:448
  36.1 0.0 copy-start.1
  36.1 1.2 %copy-done.1 = bf16[512,1024]{1,0:T(8,128)(2,1)S(1)} copy-done((bf16[512,1024]{1,0:T(8,128)(2,1)S(1)}, bf16[512,1024]{1,0:T(8,128)(2,1)}, u32[]{:S(2)}) %copy-start.1) | copy-done | bytes 1048600
  37.3 1.2 %shard_map.115 = (f32[16,128]{1,0:T(8,128)S(1)}, s32[4]{0:T(128)S(1)}, bf16[512,1024]{1,0:T(8,128)(2,1)S(1)}) custom-call(f32[8,128]{1,0:T(8,128)S(1)} %collective-permute-done.before_ref, f32[8,128]{1,0:T(8,128)S(1)} %get-tuple-element.37.docs_ref, bf16[512,1024]{1,0:T(8,128)(2,1)S(1)} %copy-done.1), custom_call_target="tpu_custom_call" | custom-call | bytes 131072 | tf_op jit(solution)/shard_map/pallas_call | solution.py:450
  38.5 7.5 %collective-permute-done.1.halo_ref = bf16[2048,128]{1,0:T(8,128)(2,1)S(1)} collective-permute-done((bf16[2048,128]{1,0:T(8,128)(2,1)}, bf16[2048,128]{1,0:T(8,128)(2,1)S(1)}, u32[]{:S(2)}, u32[]{:S(2)}) %collective-permute-start.1) | collective-permute-done | bytes 524320 | tf_op jit(solution)/shard_map/ppermute | solution.py:445
  46.0 1.5 %shard_map.116 = (f32[32,1024]{1,0:T(8,128)S(1)}, bf16[32,1024]{1,0:T(8,128)(2,1)S(1)}) custom-call(bf16[8,288,128]{2,1,0:T(8,128)(2,1)S(1)} %all-to-all-done.own_ref, bf16[2048,128]{1,0:T(8,128)(2,1)S(1)} %collective-permute-done.1.halo_ref, f32[8,128]{1,0:T(8,128)S(1)} %collective-permute-done.before_ref, f32[8,128]{1,0:T(8,128)S(1)} %get-tuple-element.37.docs_ref, ...), custom_call_target="tpu_custom_call" | custom-call | flops 16106127360 | bytes 4194304 | tf_op jit(solution)/shard_map/pallas_call | solution.py:464
  47.6 3.4 %collective-permute-start.2 = (bf16[32,1024]{1,0:T(8,128)(2,1)S(1)}, bf16[32,1024]{1,0:T(8,128)(2,1)S(1)}, u32[]{:S(2)}, u32[]{:S(2)}) collective-permute-start(bf16[32,1024]{1,0:T(8,128)(2,1)S(1)} %get-tuple-element.46), channel_id=1, source_target_pairs={{0,1},{1,0},{2,3},{3,2},{4,5},{5,4},{6,7},{7,6},{8,9},{9,8},{10,11... | collective-permute-start | bytes 196616 | tf_op jit(solution)/shard_map/ppermute | solution.py:475
  50.9 0.9 collective-permute-done.2.came_ref
  51.8 0.7 shard_map.117
  52.5 3.4 %all-to-all-start.2 = ((bf16[4,32,1024]{2,1,0:T(8,128)(2,1)}), bf16[4,32,1024]{2,1,0:T(8,128)(2,1)S(1)}, u32[]{:S(2)}, u32[]{:S(2)}) async-start(bf16[4,32,1024]{2,1,0:T(8,128)(2,1)} %shard_map.117), calls=%async_computation.2 | async-start | bytes 524288 | tf_op jit(solution)/shard_map/all_to_all | solution.py:485
  56.0 0.0 copy-start.2
  56.0 3.3 %shard_map.118.refs_0_ = bf16[1024,512]{1,0:T(8,128)(2,1)} custom-call(s32[4]{0:T(128)S(1)} %get-tuple-element.54.low_ref, bf16[1024,512]{1,0:T(8,128)(2,1)} %bitcast.5.queries_ref, bf16[8,288,128]{2,1,0:T(8,128)(2,1)S(1)} %all-to-all-done.own_ref, bf16[2048,128]{1,0:T(8,128)(2,1)S(1)} %collective-permute-done.1.halo_ref, ...), custom_call_target="tpu_custom_call" | custom-call | flops 1610612736 | bytes 2097152 | tf_op jit(solution)/shard_map/pallas_call | solution.py:366
  59.2 2.8 %all-to-all-done.2.parts_ref = bf16[4,32,1024]{2,1,0:T(8,128)(2,1)S(1)} async-done(((bf16[4,32,1024]{2,1,0:T(8,128)(2,1)}), bf16[4,32,1024]{2,1,0:T(8,128)(2,1)S(1)}, u32[]{:S(2)}, u32[]{:S(2)}) %all-to-all-start.2) | async-done | bytes 262176 | tf_op jit(solution)/shard_map/all_to_all | solution.py:485
  62.1 1.4 %shard_map.119 = f32[8,8,128]{2,1,0:T(8,128)} custom-call(bf16[4,32,1024]{2,1,0:T(8,128)(2,1)S(1)} %all-to-all-done.2.parts_ref, f32[1,1024]{1,0:T(1,128)S(1)} %bitcast.18, bf16[2,1024,256]{2,1,0:T(8,128)(2,1)S(1)} %copy-done, bf16[2,1024,256]{2,1,0:T(8,128)(2,1)S(1)} %collective-permute-done.3.other_ref, f32[8,128]{1,0:T(8,128)S(1)} %get-tuple-element.53.info_ref), custom_call_target="tpu_custom_call" | custom-call | flops 134217728 | bytes 2097152 | tf_op jit(solution)/shard_map/pallas_call | solution.py:499
  63.4 4.7 %all-to-all-start.3 = ((f32[8,8,128]{2,1,0:T(8,128)}), f32[8,8,128]{2,1,0:T(8,128)S(1)}, u32[]{:S(2)}, u32[]{:S(2)}) async-start(f32[8,8,128]{2,1,0:T(8,128)} %shard_map.119), calls=%async_computation.3 | async-start | bytes 65536 | tf_op jit(solution)/shard_map/all_to_all | solution.py:385
  68.2 4.8 %shard_map.120 = bf16[1024,512]{1,0:T(8,128)(2,1)} custom-call(s32[4]{0:T(128)S(1)} %get-tuple-element.54.low_ref, bf16[1024,512]{1,0:T(8,128)(2,1)} %bitcast.5.queries_ref, bf16[8,288,128]{2,1,0:T(8,128)(2,1)S(1)} %all-to-all-done.own_ref, bf16[2048,128]{1,0:T(8,128)(2,1)S(1)} %collective-permute-done.1.halo_ref, ...), custom_call_target="tpu_custom_call", output_to_operand_aliasing={{}: (5, {})} | custom-call | flops 1610612736 | bytes 2097152 | tf_op jit(solution)/shard_map/pallas_call | solution.py:366
  73.0 0.3 shard_map.121
  73.2 23.1 %all_to_all.29 = f32[64,1,128]{2,1,0:T(1,128)S(1)} all-to-all(f32[64,1,128]{2,1,0:T(1,128)S(1)} %bitcast.17), channel_id=1, replica_groups=mesh['ctx'=64,'head'=8] {'ctx'}, dimensions={0} | all-to-all | bytes 65536 | tf_op jit(solution)/shard_map/all_to_all | solution.py:529
  96.3 0.6 reduce_sum.9
  (13 shorter events, 0.0 us)
Async XLA Ops:
  3.8 10.5 %copy-start.6 = (s32[64,1]{0,1:T(1,128)S(1)}, s32[64,1]{0,1:T(1,128)}, u32[]{:S(2)}) copy-start(s32[64,1]{0,1:T(1,128)} %param.15) | copy-start | bytes 772
  3.8 13.8 %copy-start.7 = (bf16[128,4096]{1,0:T(8,128)(2,1)S(1)}, bf16[128,4096]{1,0:T(8,128)(2,1)}, u32[]{:S(2)}) copy-start(bf16[128,4096]{1,0:T(8,128)(2,1)} %queries_hbm.1) | copy-start | bytes 3145732
  3.8 21.8 %all-to-all-start = ((bf16[8,288,128]{2,1,0:T(8,128)(2,1)}), bf16[8,288,128]{2,1,0:T(8,128)(2,1)S(1)}, u32[]{:S(2)}, u32[]{:S(2)}) async-start(bf16[8,288,128]{2,1,0:T(8,128)(2,1)} %shard_map.113), calls=%async_computation | async-start | bytes 1179648 | tf_op jit(solution)/shard_map/all_to_all | solution.py:385
  14.3 0.7 copy-start.3
  14.3 0.7 copy-start.4
  14.3 0.7 copy-start.5
  15.6 10.0 %collective-permute-start = (f32[8,128]{1,0:T(8,128)S(1)}, f32[8,128]{1,0:T(8,128)S(1)}, u32[]{:S(2)}, u32[]{:S(2)}) collective-permute-start(f32[8,128]{1,0:T(8,128)S(1)} %get-tuple-element.33), channel_id=1, source_target_pairs={{0,8},{8,16},{16,24},{24,32},{32,40},{40,48},{48,56},{56,64},{64,7... | collective-permute-start | bytes 12296 | tf_op jit(solution)/shard_map/ppermute | solution.py:442
  26.4 7.7 %copy-start = (bf16[2,1024,256]{2,1,0:T(8,128)(2,1)S(1)}, bf16[2,1024,256]{2,1,0:T(8,128)(2,1)}, u32[]{:S(2)}) copy-start(bf16[2,1024,256]{2,1,0:T(8,128)(2,1)} %codes_ref.1) | copy-start | bytes 3145732
  26.4 19.6 %collective-permute-start.1 = (bf16[2048,128]{1,0:T(8,128)(2,1)}, bf16[2048,128]{1,0:T(8,128)(2,1)S(1)}, u32[]{:S(2)}, u32[]{:S(2)}) collective-permute-start(bf16[2048,128]{1,0:T(8,128)(2,1)} %bitcast.4), channel_id=1, source_target_pairs={{0,8},{8,16},{16,24},{24,32},{32,40},{40,48},{48,56},{56,64},{64,7... | collective-permute-start | bytes 1572872 | tf_op jit(solution)/shard_map/ppermute | solution.py:445
  28.5 24.1 %all-to-all-start.1 = ((bf16[8,128,512]{2,1,0:T(8,128)(2,1)}), bf16[8,128,512]{2,1,0:T(8,128)(2,1)}, u32[]{:S(2)}, u32[]{:S(2)}) async-start(bf16[8,128,512]{2,1,0:T(8,128)(2,1)} %bitcast.16), calls=%async_computation.1 | async-start | bytes 2097152 | tf_op jit(solution)/shard_map/all_to_all | solution.py:385
  34.2 27.9 %collective-permute-start.3 = (bf16[2,1024,256]{2,1,0:T(8,128)(2,1)S(1)}, bf16[2,1024,256]{2,1,0:T(8,128)(2,1)S(1)}, u32[]{:S(2)}, u32[]{:S(2)}) collective-permute-start(bf16[2,1024,256]{2,1,0:T(8,128)(2,1)S(1)} %copy-done), channel_id=1, source_target_pairs={{0,1},{1,0},{2,3},{3,2},{4,5},{5,4},{6,7},{7,6},{8,9},{9,8},{10,11... | collective-permute-start | bytes 3145736 | tf_op jit(solution)/shard_map/ppermute | solution.py:448
  36.1 1.2 %copy-start.1 = (bf16[512,1024]{1,0:T(8,128)(2,1)S(1)}, bf16[512,1024]{1,0:T(8,128)(2,1)}, u32[]{:S(2)}) copy-start(bf16[512,1024]{1,0:T(8,128)(2,1)} %proj_hbm) | copy-start | bytes 3145732
  47.6 4.2 %collective-permute-start.2 = (bf16[32,1024]{1,0:T(8,128)(2,1)S(1)}, bf16[32,1024]{1,0:T(8,128)(2,1)S(1)}, u32[]{:S(2)}, u32[]{:S(2)}) collective-permute-start(bf16[32,1024]{1,0:T(8,128)(2,1)S(1)} %get-tuple-element.46), channel_id=1, source_target_pairs={{0,1},{1,0},{2,3},{3,2},{4,5},{5,4},{6,7},{7,6},{8,9},{9,8},{10,11... | collective-permute-start | bytes 196616 | tf_op jit(solution)/shard_map/ppermute | solution.py:475
  52.5 9.5 %all-to-all-start.2 = ((bf16[4,32,1024]{2,1,0:T(8,128)(2,1)}), bf16[4,32,1024]{2,1,0:T(8,128)(2,1)S(1)}, u32[]{:S(2)}, u32[]{:S(2)}) async-start(bf16[4,32,1024]{2,1,0:T(8,128)(2,1)} %shard_map.117), calls=%async_computation.2 | async-start | bytes 524288 | tf_op jit(solution)/shard_map/all_to_all | solution.py:485
  56.0 6.1 %copy-start.2 = (f32[1024]{0:T(1024)S(1)}, f32[1024]{0:T(1024)}, u32[]{:S(2)}) copy-start(f32[1024]{0:T(1024)} %param.18) | copy-start | bytes 12292
  63.4 9.5 %all-to-all-start.3 = ((f32[8,8,128]{2,1,0:T(8,128)}), f32[8,8,128]{2,1,0:T(8,128)S(1)}, u32[]{:S(2)}, u32[]{:S(2)}) async-start(f32[8,8,128]{2,1,0:T(8,128)} %shard_map.119), calls=%async_computation.3 | async-start | bytes 65536 | tf_op jit(solution)/shard_map/all_to_all | solution.py:385
